TPU v7x, 32 devices: a whole 2x2x4 slice. The times are simulated.
32 devices in a mesh: rows: 8 (over z, x), cols: 4 (over y, core).
Axes of the slice: x: 2, y: 2, z: 4, core: 2. Of those that a mesh axis runs over, the one named last changes fastest.
Arguments:
- matrix: bfloat16 [16384, 1024], P('rows', 'cols'), as said below
- row_signs: int32 [16384], P('rows'), may hold values from 0 to 1
- sampled_rows: int32 [8, 2048], P('rows'), may hold values from 0 to 2047
- right_sides: float32 [8, 16384], P(None, 'rows'), may hold values from -6 to 6
Outputs:
- solution: float32 [8, 1024], P(None, 'cols')
- residual: float32 [8, 16384], P(None, 'rows')
Inputs may be any that keep to these rules, and one draw needn't show every extreme that they name: `matrix`: entries are at most 70 / sqrt(16384) in magnitude.
All inputs are finite; a program needn't handle non-finite values.
Results may differ from a plain program's by a relative error of at most 0.0013.
Values sent between devices are 32-bit elements; how exact they have to be, the bound alone decides.
A program may use at most 64 MiB of HBM per device.

v0:
```python
import math

import jax
import jax.numpy as jnp
from jax import lax
from jax.sharding import PartitionSpec as P

SKETCH = 2048
ROUNDS = 2


highest = lax.Precision.HIGHEST


def sylvester(matrix_order):
    positions = jnp.arange(matrix_order, dtype=jnp.int32)
    common = jnp.bitwise_and(positions[:, None], positions[None, :])
    parity = jnp.zeros((matrix_order, matrix_order), jnp.int32)
    for bit_place in range(max(matrix_order.bit_length() - 1, 0)):
        parity = parity + jnp.bitwise_and(jnp.right_shift(common, bit_place), 1)
    return jnp.where(jnp.bitwise_and(parity, 1) == 0, 1.0, -1.0).astype(jnp.float32)


def transform(signed):
    row_count, col_count = signed.shape
    bit_count = row_count.bit_length() - 1
    outer_order = 2 ** (bit_count - bit_count // 2)
    inner_order = row_count // outer_order
    section_one = jnp.dot(
        sylvester(outer_order).astype(jnp.bfloat16),
        signed.reshape(outer_order, inner_order * col_count),
        preferred_element_type=jnp.float32,
    )
    second = jnp.einsum(
        "cd,adn->acn",
        sylvester(inner_order),
        section_one.reshape(outer_order, inner_order, col_count),
        precision=highest,
    )
    return second.reshape(row_count, col_count)


def solve_right(factor, vectors):
    return lax.linalg.triangular_solve(
        factor, vectors, left_side=False, lower=True, transpose_a=True
    )


def solve_left(factor, vectors):
    return lax.linalg.triangular_solve(
        factor, vectors, left_side=False, lower=True, transpose_a=False
    )


def local(matrix, row_signs, sampled_rows, right_sides):
    row_count, col_count = matrix.shape
    systems = right_sides.shape[0]
    flipped = (1 - 2 * row_signs).astype(jnp.bfloat16)
    signed = matrix * flipped[:, None]
    mixed_rows = transform(signed)
    picked = jnp.take(mixed_rows, sampled_rows[0], axis=0) * (1.0 / math.sqrt(SKETCH))
    sketch_piece = lax.psum_scatter(picked, "rows", scatter_dimension=0, tiled=True)
    gram_block = lax.dot_general(
        lax.all_gather(sketch_piece, "cols", axis=1, tiled=True),
        sketch_piece,
        (((0,), (0,)), ((), ())),
        precision=highest,
    )
    gram_summed = lax.psum(gram_block, "rows")
    gram_matrix = lax.all_gather(gram_summed, "cols", axis=1, tiled=True)
    factor = jnp.linalg.cholesky(gram_matrix)
    col_start = lax.axis_index("cols") * col_count

    def forward(vectors):
        own_part = lax.dynamic_slice_in_dim(vectors, col_start, col_count, 1)
        local_part = lax.dot_general(
            own_part, matrix.astype(jnp.float32), (((1,), (1,)), ((), ())), precision=highest
        )
        return lax.psum(local_part, "cols")

    def back_section(forward_rest):
        local_squares = jnp.sum(forward_rest * forward_rest, axis=1)
        local_part = jnp.dot(forward_rest, matrix.astype(jnp.float32), precision=highest)
        summed, total_squares = lax.psum((local_part, local_squares), "rows")
        beta_norm = jnp.sqrt(total_squares)
        summed = summed / beta_norm[:, None]
        left_unit = forward_rest / beta_norm[:, None]
        whole_vector = lax.all_gather(summed, "cols", axis=1, tiled=True)
        return (beta_norm, left_unit, solve_right(factor, whole_vector))

    beta_norm, left_unit, back_rest = back_section(right_sides)
    alpha_norm = jnp.sqrt(jnp.sum(back_rest * back_rest, axis=1))
    right_unit = back_rest / alpha_norm[:, None]
    search = right_unit
    coeffs = jnp.zeros((systems, back_rest.shape[1]), jnp.float32)
    phibar = beta_norm
    rhobar = alpha_norm
    for iteration in range(ROUNDS):
        forward_rest = forward(solve_left(factor, right_unit)) - alpha_norm[:, None] * left_unit
        beta_norm, left_unit, back_rest = back_section(forward_rest)
        back_rest = back_rest - beta_norm[:, None] * right_unit
        alpha_norm = jnp.sqrt(jnp.sum(back_rest * back_rest, axis=1))
        right_unit = back_rest / alpha_norm[:, None]
        rho_total = jnp.sqrt(rhobar * rhobar + beta_norm * beta_norm)
        cosine = rhobar / rho_total
        sine_part = beta_norm / rho_total
        theta_term = sine_part * alpha_norm
        rhobar = -cosine * alpha_norm
        phi_term = cosine * phibar
        phibar = sine_part * phibar
        coeffs = coeffs + (phi_term / rho_total)[:, None] * search
        search = right_unit - (theta_term / rho_total)[:, None] * search
    full_solution = solve_left(factor, coeffs)
    residual = right_sides - forward(full_solution)
    solution = lax.dynamic_slice_in_dim(full_solution, col_start, col_count, 1)
    return (solution, residual)


def solution(mesh):
    in_specs = (P("rows", "cols"), P("rows"), P("rows", None), P(None, "rows"))
    out_specs = (P(None, "cols"), P(None, "rows"))
    return jax.shard_map(local, mesh=mesh, in_specs=in_specs, out_specs=out_specs, check_vma=False)
```

profile of v0, /device:TPU:0, one launch (start us, length us, event | category | flops | bytes accessed | tf_op | source)
XLA Modules:
  0.0 756.2 jit_solution(9592627670413790413)
XLA Ops:
  7.9 1.6 broadcast_multiply_fusion
  10.5 3.2 fusion.1
  13.7 8.6 %gather_fusion = f32[2048,256]{1,0:T(8,128)} fusion(f32[2048,256]{1,0:T(8,128)S(1)} %bitcast.306, s32[2048]{0:T(1024)S(1)} %broadcast_clamp_fusion), kind=kCustom, calls=%fused_computation | custom fusion | bytes 4202496 | tf_op jit(solution)/shard_map/jit(_take)/gather | solution.py:61
  22.3 2.8 select_multiply_fusion
  25.2 71.1 %reduce-scatter.2.cloned.1.call-done = f32[256,256]{1,0:T(8,128)} async-done(((f32[2048,256]{1,0:T(8,128)}), f32[256,256]{1,0:T(8,128)}) %reduce-scatter.2.cloned.1.call-update) | async-done | bytes 262160 | tf_op jit(solution)/shard_map/reduce_scatter | solution.py:62
  96.4 17.2 %all-gather.3.cloned.1.call-done = f32[256,1024]{1,0:T(8,128)} async-done(((f32[256,256]{1,0:T(8,128)}), f32[256,1024]{1,0:T(8,128)}) %all-gather.3.cloned.1.call-update) | async-done | bytes 1048592 | tf_op jit(solution)/shard_map/all_gather | solution.py:64
  113.6 3.3 fusion.239
  117.0 78.3 %all-reduce.8.cloned.1.call-done = f32[1024,256]{0,1:T(8,128)} async-done(((f32[1024,256]{0,1:T(8,128)}), f32[1024,256]{0,1:T(8,128)}) %all-reduce.8.cloned.1.call-update) | async-done | bytes 1048592 | tf_op jit(solution)/shard_map/psum | solution.py:69
  196.0 20.6 %all-reduce.2 = (f32[8,256]{1,0:T(8,128)S(1)}, f32[8]{0:T(128)S(1)}) all-reduce(f32[8,256]{1,0:T(8,128)S(1)} %fusion.240, f32[8]{0:T(128)S(1)} %multiply_reduce_fusion.2), channel_id=1, replica_groups=mesh['rows'=8,'cols'=4] {'rows'}, use_global_device_ids=true, to_apply=%region_18.19 | all-reduce | flops 2056 | bytes 16448 | tf_op jit(solution)/shard_map/psum | solution.py:84
  216.7 5.3 all_gather.14
  222.0 9.0 %all-gather.5.cloned.1.call-done = f32[1024,1024]{0,1:T(8,128)} async-done(((f32[1024,256]{0,1:T(8,128)}), f32[1024,1024]{0,1:T(8,128)}) %all-gather.5.cloned.1.call-update) | async-done | bytes 4194320 | tf_op jit(solution)/shard_map/all_gather | solution.py:70
  231.1 5.5 copy.9
  236.6 4.4 fusion
  241.0 1.9 copy-done.1
  242.9 11.7 %cholesky.223 = f32[128,128]{1,0:T(8,128)S(1)} custom-call(f32[128,128]{1,0:T(8,128)S(1)} %cholesky.580), custom_call_target="Cholesky" | custom-call | tf_op jit(solution)/shard_map/jit(cholesky)/cholesky | solution.py:71
  254.7 9.8 %custom-call.65 = f32[1,128,128]{1,2,0:T(8,128)S(1)} custom-call(f32[1,128,128]{2,1,0:T(8,128)S(1)} %get-tuple-element.85), custom_call_target="InvertDiagBlocksLowerTriangular" | custom-call | tf_op jit(solution)/shard_map/jit(cholesky)/cholesky | solution.py:71
  264.5 2.5 cholesky.255
  267.0 2.4 constant_dynamic-update-slice_fusion.129
  269.4 1.5 convolution_subtract_fusion
  270.9 11.9 %cholesky.244 = f32[128,128]{1,0:T(8,128)S(1)} custom-call(f32[128,128]{1,0:T(8,128)S(1)} %cholesky.584), custom_call_target="Cholesky" | custom-call | tf_op jit(solution)/shard_map/jit(cholesky)/cholesky | solution.py:71
  283.5 9.8 %custom-call.66 = f32[1,128,128]{1,2,0:T(8,128)S(1)} custom-call(f32[1,128,128]{2,1,0:T(8,128)S(1)} %get-tuple-element.82), custom_call_target="InvertDiagBlocksLowerTriangular" | custom-call | tf_op jit(solution)/shard_map/jit(cholesky)/cholesky | solution.py:71
  294.5 2.1 convolution_subtract_fusion.1
  296.7 11.7 %cholesky.468 = f32[128,128]{1,0:T(8,128)S(1)} custom-call(f32[128,128]{1,0:T(8,128)S(1)} %cholesky.589), custom_call_target="Cholesky" | custom-call | tf_op jit(solution)/shard_map/jit(cholesky)/cholesky | solution.py:71
  309.6 9.8 %custom-call.67 = f32[1,128,128]{1,2,0:T(8,128)S(1)} custom-call(f32[1,128,128]{2,1,0:T(8,128)S(1)} %get-tuple-element.79), custom_call_target="InvertDiagBlocksLowerTriangular" | custom-call | tf_op jit(solution)/shard_map/jit(cholesky)/cholesky | solution.py:71
  320.6 2.3 convolution_subtract_fusion.2
  323.0 12.1 %cholesky.487 = f32[128,128]{1,0:T(8,128)S(1)} custom-call(f32[128,128]{1,0:T(8,128)S(1)} %cholesky.594), custom_call_target="Cholesky" | custom-call | tf_op jit(solution)/shard_map/jit(cholesky)/cholesky | solution.py:71
  336.3 9.8 %custom-call.68 = f32[1,128,128]{1,2,0:T(8,128)S(1)} custom-call(f32[1,128,128]{2,1,0:T(8,128)S(1)} %get-tuple-element.76), custom_call_target="InvertDiagBlocksLowerTriangular" | custom-call | tf_op jit(solution)/shard_map/jit(cholesky)/cholesky | solution.py:71
  347.2 2.3 convolution_subtract_fusion.3
  349.6 11.7 %cholesky.506 = f32[128,128]{1,0:T(8,128)S(1)} custom-call(f32[128,128]{1,0:T(8,128)S(1)} %cholesky.599), custom_call_target="Cholesky" | custom-call | tf_op jit(solution)/shard_map/jit(cholesky)/cholesky | solution.py:71
  362.6 9.9 %custom-call.69 = f32[1,128,128]{1,2,0:T(8,128)S(1)} custom-call(f32[1,128,128]{2,1,0:T(8,128)S(1)} %get-tuple-element.73), custom_call_target="InvertDiagBlocksLowerTriangular" | custom-call | tf_op jit(solution)/shard_map/jit(cholesky)/cholesky | solution.py:71
  373.6 2.3 convolution_subtract_fusion.4
  375.9 11.7 %cholesky.526 = f32[128,128]{1,0:T(8,128)S(1)} custom-call(f32[128,128]{1,0:T(8,128)S(1)} %cholesky.604), custom_call_target="Cholesky" | custom-call | tf_op jit(solution)/shard_map/jit(cholesky)/cholesky | solution.py:71
  388.9 9.8 %custom-call.70 = f32[1,128,128]{1,2,0:T(8,128)S(1)} custom-call(f32[1,128,128]{2,1,0:T(8,128)S(1)} %get-tuple-element.70), custom_call_target="InvertDiagBlocksLowerTriangular" | custom-call | tf_op jit(solution)/shard_map/jit(cholesky)/cholesky | solution.py:71
  399.6 2.0 convolution_subtract_fusion.5
  401.7 11.9 %cholesky.546 = f32[128,128]{1,0:T(8,128)S(1)} custom-call(f32[128,128]{1,0:T(8,128)S(1)} %cholesky.609), custom_call_target="Cholesky" | custom-call | tf_op jit(solution)/shard_map/jit(cholesky)/cholesky | solution.py:71
  414.8 9.8 %custom-call.71 = f32[1,128,128]{1,2,0:T(8,128)S(1)} custom-call(f32[1,128,128]{2,1,0:T(8,128)S(1)} %get-tuple-element.67), custom_call_target="InvertDiagBlocksLowerTriangular" | custom-call | tf_op jit(solution)/shard_map/jit(cholesky)/cholesky | solution.py:71
  425.5 1.8 convolution_subtract_fusion.6
  427.2 11.7 %cholesky.564 = f32[128,128]{1,0:T(8,128)S(1)} custom-call(f32[128,128]{1,0:T(8,128)S(1)} %convolution_subtract_fusion.6), custom_call_target="Cholesky" | custom-call | tf_op jit(solution)/shard_map/jit(cholesky)/cholesky | solution.py:71
  445.8 4.8 select_select_fusion
  450.6 23.0 %while.10 = (s32[]{:T(128)}, f32[1024,1024]{1,0:T(8,128)}, s32[8,2]{0,1:T(2,128)S(1)}, f32[8,128,128]{2,1,0:T(8,128)S(1)}, s32[]{:T(128)}) while((s32[]{:T(128)}, f32[1024,1024]{1,0:T(8,128)}, s32[8,2]{0,1:T(2,128)S(1)}, f32[8,128,128]{2,1,0:T(8,128)S(1)}, s32[]{:T(128)}) %tuple.113), condition=%wide.while_cond, body=%wide.while_body.sunk | while | flops 2 | bytes 131181 | solution.py:44
  451.2 2.3 bitcast_dynamic-update-slice_fusion.2
  454.1 2.3 bitcast_dynamic-update-slice_fusion.2
  456.9 2.3 bitcast_dynamic-update-slice_fusion.2
  459.8 2.3 bitcast_dynamic-update-slice_fusion.2
  462.7 2.3 bitcast_dynamic-update-slice_fusion.2
  465.6 2.3 bitcast_dynamic-update-slice_fusion.2
  468.5 2.3 bitcast_dynamic-update-slice_fusion.2
  471.4 2.2 bitcast_dynamic-update-slice_fusion.2
  473.6 78.8 %custom-call.75 = f32[8,128,128]{1,2,0:T(8,128)S(1)} custom-call(f32[8,128,128]{2,1,0:T(8,128)S(1)} %get-tuple-element.38), custom_call_target="InvertDiagBlocksLowerTriangular" | custom-call | tf_op jit(solution)/shard_map/triangular_solve/custom-call.7 | solution.py:44
  558.0 1.4 convolution_subtract_fusion.27
  559.5 1.4 convolution_subtract_fusion.41
  561.1 1.5 convolution_subtract_fusion.40
  573.4 1.6 fusion.192
  575.1 31.2 %all-reduce.10.cloned.1.call-done = f32[8,2048]{1,0:T(8,128)} async-done(((f32[8,2048]{1,0:T(8,128)}), f32[8,2048]{1,0:T(8,128)}) %all-reduce.10.cloned.1.call-update) | async-done | bytes 65552 | tf_op jit(solution)/shard_map/psum | solution.py:79
  607.8 21.8 %all-reduce.1 = (f32[8,256]{1,0:T(8,128)S(1)}, f32[8]{0:T(128)S(1)}) all-reduce(f32[8,256]{1,0:T(8,128)S(1)} %fusion.241, f32[8]{0:T(128)S(1)} %get-tuple-element.60), channel_id=1, replica_groups=mesh['rows'=8,'cols'=4] {'rows'}, use_global_device_ids=true, to_apply=%region_25.28 | all-reduce | flops 2056 | bytes 16448 | tf_op jit(solution)/shard_map/psum | solution.py:84
  629.7 5.2 all_gather.15
  642.1 1.4 convolution_subtract_fusion.37
  643.7 1.5 convolution_subtract_fusion.36
  656.0 1.6 fusion.190
  657.7 27.5 %all-reduce.12.cloned.1.call-done = f32[8,2048]{1,0:T(8,128)} async-done(((f32[8,2048]{1,0:T(8,128)}), f32[8,2048]{1,0:T(8,128)}) %all-reduce.12.cloned.1.call-update) | async-done | bytes 65552 | tf_op jit(solution)/shard_map/psum | solution.py:79
  686.2 21.6 %psum.70 = f32[8]{0:T(128)S(1)} all-reduce(f32[8]{0:T(128)S(1)} %multiply_reduce_fusion), channel_id=1, replica_groups=mesh['rows'=8,'cols'=4] {'rows'}, use_global_device_ids=true, to_apply=%region_29.32 | all-reduce | flops 8 | bytes 64 | tf_op jit(solution)/shard_map/psum | solution.py:84
  718.3 1.6 fusion.242
  719.9 27.5 %all-reduce.14.cloned.1.call-done = f32[8,2048]{1,0:T(8,128)} async-done(((f32[8,2048]{1,0:T(8,128)}), f32[8,2048]{1,0:T(8,128)}) %all-reduce.14.cloned.1.call-update) | async-done | bytes 65552 | tf_op jit(solution)/shard_map/psum | solution.py:79
  747.3 1.5 sub.27
  (231 shorter events, 70.4 us)
Async XLA Ops:
  7.2 89.1 %reduce-scatter.2.cloned.1.call-start = ((), (), s32[]{:S(2)}) async-start(), calls=%async_computation.1 | async-start | bytes 2359296 | tf_op jit(solution)/shard_map/reduce_scatter | solution.py:62
  10.0 3.7 copy-start.4
  25.1 170.3 %copy-start.2 = (f32[8,2048]{1,0:T(8,128)S(1)}, f32[8,2048]{1,0:T(8,128)}, u32[]{:S(2)}) copy-start(f32[8,2048]{1,0:T(8,128)} %param.11) | copy-start | bytes 196612
  25.1 170.4 %copy-start = (bf16[2048,256]{1,0:T(8,128)(2,1)S(1)}, bf16[2048,256]{1,0:T(8,128)(2,1)}, u32[]{:S(2)}) copy-start(bf16[2048,256]{1,0:T(8,128)(2,1)} %param.8) | copy-start | bytes 3145732
  25.1 88.5 %all-gather.3.cloned.1.call-start = ((), (), s32[]{:S(2)}) async-start(), calls=%async_computation.2 | async-start | bytes 1310720 | tf_op jit(solution)/shard_map/all_gather | solution.py:64
  96.3 99.0 %all-reduce.8.cloned.1.call-start = ((), (), s32[]{:S(2)}) async-start(), calls=%async_computation.3 | async-start | bytes 2097152 | tf_op jit(solution)/shard_map/psum | solution.py:69
  117.0 114.1 %all-gather.5.cloned.1.call-start = ((), (), s32[]{:S(2)}) async-start(), calls=%async_computation.4 | async-start | bytes 5242880 | tf_op jit(solution)/shard_map/all_gather | solution.py:70
  195.3 410.9 %all-reduce.10.cloned.1.call-start = ((), (), s32[]{:S(2)}) async-start(), calls=%async_computation.5 | async-start | bytes 131072 | tf_op jit(solution)/shard_map/psum | solution.py:79
  241.0 1.9 copy-start.1
  575.0 110.1 %all-reduce.12.cloned.1.call-start = ((), (), s32[]{:S(2)}) async-start(), calls=%async_computation.6 | async-start | bytes 131072 | tf_op jit(solution)/shard_map/psum | solution.py:79
  657.6 89.7 %all-reduce.14.cloned.1.call-start = ((), (), s32[]{:S(2)}) async-start(), calls=%async_computation.7 | async-start | bytes 131072 | tf_op jit(solution)/shard_map/psum | solution.py:79
  718.3 30.5 %copy-start.3 = (f32[8,256]{1,0:T(8,128)}, f32[8,256]{1,0:T(8,128)S(1)}, u32[]{:S(2)}) copy-start(f32[8,256]{1,0:T(8,128)S(1)} %constant_dynamic-slice_fusion.1) | copy-start | bytes 24580
Sparse Core Ops, SparseCore 0:
  25.2 71.0 reduce-scatter.1
  97.8 15.7 all-gather.2
  117.1 78.1 all-reduce.7
  196.8 34.2 all-gather.4
  575.1 31.0 all-reduce.9
  657.7 27.3 all-reduce.11
  720.0 27.3 all-reduce.13
where the time goes:
time: 764 us; the launch traced here: 756 us
  other arithmetic  270 us (35%)
  waiting for transfers between devices  262 us (34%)
  matrix products  86.6 us (11%)
  blocking collectives  74.6 us (10%)
  local copies, waits for them, and re-layouts  42.4 us (6%)
  between operations  20.4 us (3%)
    another operation x30, other arithmetic, local(): factor = jnp.linalg.cholesky(gram_matrix)  172 us
    psum x3, waiting for transfers between devices, forward(): return lax.psum(local_part, 'cols')  86.1 us
    another operation x4, other arithmetic, solve_right(): lax.linalg.triangular_solve(factor, vectors, left_side=False, lower=True,...  83.6 us
    psum x1, waiting for transfers between devices, local(): gram_summed = lax.psum(gram_block, 'rows')  78.3 us
    reduce_scatter x1, waiting for transfers between devices, local(): lax.psum_scatter(picked, 'rows', scatter_dimension=0, tiled=True)  71.1 us
    psum x3, blocking collectives, back_section(): summed, total_squares = lax.psum((local_part, local_squares), 'rows')  64 us
    another operation x45, matrix products, solve_left(): lax.linalg.triangular_solve(factor, vectors, left_side=False, lower=True,...  30 us
    another operation x14, matrix products, local(): factor = jnp.linalg.cholesky(gram_matrix)  23.1 us
  transfers between devices with their start and end apart: 7, of which 7 were waited for; matrix products, arithmetic and copies ran while one was open for 0% of the time, Pallas kernels for 0%

commit v1 on v0

v1 whole, which is shorter than its diff:
```python
import functools
import math

import jax
import jax.numpy as jnp
from jax import lax
from jax.experimental import pallas as pl
from jax.experimental.pallas import tpu as pltpu
from jax.sharding import PartitionSpec as P

ROUNDS = 2
BLOCK = 128
STRIP = 8

highest = lax.Precision.HIGHEST


def sylvester(matrix_order):
    positions = jnp.arange(matrix_order, dtype=jnp.int32)
    common = jnp.bitwise_and(positions[:, None], positions[None, :])
    parity = jnp.zeros((matrix_order, matrix_order), jnp.int32)
    for bit_place in range(max(matrix_order.bit_length() - 1, 0)):
        parity = parity + jnp.bitwise_and(jnp.right_shift(common, bit_place), 1)
    return jnp.where(jnp.bitwise_and(parity, 1) == 0, 1.0, -1.0).astype(jnp.float32)


def block_inverse(square):
    size = square.shape[0]
    row_ids = lax.broadcasted_iota(jnp.int32, (size, size), 0)
    col_ids = lax.broadcasted_iota(jnp.int32, (size, size), 1)
    rest = square
    unit = jnp.where(row_ids == col_ids, 1.0, 0.0).astype(jnp.float32)
    finished = []
    for strip in range(size // STRIP):
        start = strip * STRIP
        height = size - start
        here = lax.broadcasted_iota(jnp.int32, (height, size), 0)
        columns = [
            jnp.broadcast_to(rest[:, start + k:start + k + 1], (height, size)) for k in range(STRIP)
        ]
        scale = jnp.ones((STRIP, size), jnp.float32)
        for k in range(STRIP):
            pivot = columns[k][k:k + 1, :]
            factors = jnp.where(here > k, columns[k] * (1.0 / pivot), 0.0)
            for later in range(k + 1, STRIP):
                columns[later] = columns[later] - factors * columns[later][k:k + 1, :]
            rest = rest - factors * rest[k:k + 1, :]
            unit = unit - factors * unit[k:k + 1, :]
            scale = jnp.where(here[:STRIP] == k, lax.rsqrt(pivot), scale)
        finished.append(unit[:STRIP] * scale)
        rest = rest[STRIP:]
        unit = unit[STRIP:]
    return jnp.concatenate(finished, axis=0)


def inverse_factor_kernel(gram_ref, out_ref, strip_ref):
    order = gram_ref.shape[0]
    blocks = order // BLOCK
    out_ref[...] = gram_ref[...]

    def step(block, carry):
        start = pl.multiple_of(block * BLOCK, BLOCK)
        own = pl.ds(start, BLOCK)
        inverse = block_inverse(out_ref[own, own])
        strip_ref[...] = jnp.dot(
            inverse, out_ref[own, :], precision=highest, preferred_element_type=jnp.float32
        )
        strip_ref[:, own] = inverse

        def update(row_block, inner):
            rows = pl.ds(pl.multiple_of(row_block * BLOCK, BLOCK), BLOCK)
            out_ref[rows, own] = jnp.zeros((BLOCK, BLOCK), jnp.float32)
            out_ref[rows, :] = out_ref[rows, :] - lax.dot_general(
                strip_ref[:, rows], strip_ref[...], (((0,), (0,)), ((), ())),
                precision=highest, preferred_element_type=jnp.float32,
            )
            return inner

        lax.fori_loop(block + 1, blocks, update, 0)
        col_ids = lax.broadcasted_iota(jnp.int32, (BLOCK, order), 1)
        out_ref[own, :] = jnp.where(col_ids < start + BLOCK, strip_ref[...], 0.0)
        return carry

    lax.fori_loop(0, blocks, step, 0)


def inverse_factor(gram_matrix):
    order = gram_matrix.shape[0]
    return pl.pallas_call(
        inverse_factor_kernel,
        out_shape=jax.ShapeDtypeStruct((order, order), jnp.float32),
        in_specs=[pl.BlockSpec(memory_space=pltpu.VMEM)],
        out_specs=pl.BlockSpec(memory_space=pltpu.VMEM),
        scratch_shapes=[pltpu.VMEM((BLOCK, order), jnp.float32)],
        compiler_params=pltpu.CompilerParams(vmem_limit_bytes=32 * 1024 * 1024),
    )(gram_matrix)


def picked_mixer(sampled, row_count):
    bit_count = row_count.bit_length() - 1
    inner_order = 2 ** (bit_count // 2)
    outer_order = row_count // inner_order
    outer = jnp.take(sylvester(outer_order).astype(jnp.bfloat16), sampled // inner_order, axis=0)
    inner = jnp.take(sylvester(inner_order).astype(jnp.bfloat16), sampled % inner_order, axis=0)
    return (outer[:, :, None] * inner[:, None, :]).reshape(sampled.shape[0], row_count)


def local(matrix, row_signs, sampled_rows, right_sides):
    row_count, col_count = matrix.shape
    flipped = (1 - 2 * row_signs).astype(jnp.bfloat16)
    signed = matrix * flipped[:, None]
    picked = jnp.dot(
        picked_mixer(sampled_rows[0], row_count), signed, preferred_element_type=jnp.float32
    ) * (1.0 / math.sqrt(sampled_rows.shape[1]))
    sketch_piece = lax.psum_scatter(picked, "rows", scatter_dimension=0, tiled=True)
    gram_block = lax.dot_general(
        lax.all_gather(sketch_piece, "cols", axis=1, tiled=True),
        sketch_piece,
        (((0,), (0,)), ((), ())),
        precision=highest,
    )
    gram_summed = lax.psum(gram_block, "rows")
    gram_matrix = lax.all_gather(gram_summed, "cols", axis=1, tiled=True)
    inverse = inverse_factor(gram_matrix)
    col_start = lax.axis_index("cols") * col_count
    wide = matrix.astype(jnp.float32)

    def forward(vectors):
        own_part = lax.dynamic_slice_in_dim(vectors, col_start, col_count, 1)
        local_part = lax.dot_general(own_part, wide, (((1,), (1,)), ((), ())), precision=highest)
        return lax.psum(local_part, "cols")

    def backward(vectors):
        squares = jnp.sum(vectors * vectors, axis=1)
        local_part = jnp.dot(vectors, wide, precision=highest)
        summed, total = lax.psum((local_part, squares), "rows")
        return jnp.sqrt(total), lax.all_gather(summed, "cols", axis=1, tiled=True)

    def solve_right(vectors):
        return lax.dot_general(vectors, inverse, (((1,), (1,)), ((), ())), precision=highest)

    def solve_left(vectors):
        return jnp.dot(vectors, inverse, precision=highest)

    beta_norm, whole_vector = backward(right_sides)
    left_unit = right_sides / beta_norm[:, None]
    back_rest = solve_right(whole_vector / beta_norm[:, None])
    alpha_norm = jnp.sqrt(jnp.sum(back_rest * back_rest, axis=1))
    right_unit = back_rest / alpha_norm[:, None]
    moved = solve_left(right_unit)
    image = forward(moved)
    search, search_image = moved, image
    full_solution = jnp.zeros_like(moved)
    solution_image = jnp.zeros_like(image)
    phibar = beta_norm
    rhobar = alpha_norm
    for iteration in range(ROUNDS):
        forward_rest = image - alpha_norm[:, None] * left_unit
        if iteration < ROUNDS - 1:
            beta_norm, whole_vector = backward(forward_rest)
        else:
            beta_norm = jnp.sqrt(lax.psum(jnp.sum(forward_rest * forward_rest, axis=1), "rows"))
        rho_total = jnp.sqrt(rhobar * rhobar + beta_norm * beta_norm)
        cosine = rhobar / rho_total
        sine_part = beta_norm / rho_total
        phi_term = cosine * phibar
        ratio = (phi_term / rho_total)[:, None]
        full_solution = full_solution + ratio * search
        solution_image = solution_image + ratio * search_image
        if iteration == ROUNDS - 1:
            break
        left_unit = forward_rest / beta_norm[:, None]
        back_rest = solve_right(whole_vector / beta_norm[:, None]) - beta_norm[:, None] * right_unit
        alpha_norm = jnp.sqrt(jnp.sum(back_rest * back_rest, axis=1))
        right_unit = back_rest / alpha_norm[:, None]
        moved = solve_left(right_unit)
        image = forward(moved)
        theta_term = sine_part * alpha_norm
        rhobar = -cosine * alpha_norm
        phibar = sine_part * phibar
        shrink = (theta_term / rho_total)[:, None]
        search = moved - shrink * search
        search_image = image - shrink * search_image
    residual = right_sides - solution_image
    solution = lax.dynamic_slice_in_dim(full_solution, col_start, col_count, 1)
    return (solution, residual)


def solution(mesh):
    in_specs = (P("rows", "cols"), P("rows"), P("rows", None), P(None, "rows"))
    out_specs = (P(None, "cols"), P(None, "rows"))
    return jax.shard_map(local, mesh=mesh, in_specs=in_specs, out_specs=out_specs, check_vma=False)
```

time: 764 us -> 428 us (0.56)
  other arithmetic: 270 us -> 7.27 us
  matrix products: 86.6 us -> 26.1 us
  Pallas kernels: 0 us -> 54.9 us
  waiting for transfers between devices: 262 us -> 234 us
  local copies, waits for them, and re-layouts: 42.4 us -> 15.6 us
    another operation x34 -> x0, other arithmetic: 256 us -> none  [the longest x30 172 us: local(): factor = jnp.linalg.cholesky(gram_matrix)]
    another operation x89 -> x0, matrix products: 73.9 us -> none  [the longest x45 30 us: solve_left(): lax.linalg.triangular_solve(factor, vectors, left_side=False, lower=True,...]
    pallas_call x0 -> x1, Pallas kernels: none -> 54.9 us  [inverse_factor(): pl.pallas_call(inverse_factor_kernel, out_shape=jax.ShapeDtypeStruct((ord...]
    psum x3 -> x2, waiting for transfers between devices: 86.1 us -> 58.7 us  [forward(): return lax.psum(local_part, 'cols')]
    another operation x45 -> x0, local copies, waits for them, and re-layouts: 25.4 us -> none  [the longest x25 22.8 us: solve_right(): lax.linalg.triangular_solve(factor, vectors, left_side=False, lower=True,...]
    dot_general x7 -> x9, matrix products: 9.34 us -> 22 us  [the longest x2 9.44 us: solve_right(): lax.dot_general(vectors, inverse, (((1,), (1,)), ((), ())), precision=hig...]
  transfers between devices with their start and end apart: 7 -> 6, of which waited for: 7 -> 6; matrix products, arithmetic and copies ran while one was open for 0% -> 0% of each run, Pallas kernels for 0% -> 0%
where the time goes in v1:
time: 428 us
  waiting for transfers between devices  234 us (55%)
  blocking collectives  74.8 us (17%)
  Pallas kernels  54.9 us (13%)
  matrix products  26.1 us (6%)
  local copies, waits for them, and re-layouts  15.6 us (4%)
  between operations  14.3 us (3%)
  other arithmetic  7.27 us (2%)
    psum x1, waiting for transfers between devices, local(): gram_summed = lax.psum(gram_block, 'rows')  78.3 us
    reduce_scatter x1, waiting for transfers between devices, local(): lax.psum_scatter(picked, 'rows', scatter_dimension=0, tiled=True)  71.2 us
    psum x2, waiting for transfers between devices, forward(): return lax.psum(local_part, 'cols')  58.7 us
    pallas_call x1, Pallas kernels, inverse_factor(): pl.pallas_call(inverse_factor_kernel, out_shape=jax.ShapeDtypeStruct((ord...  54.9 us
    psum x2, blocking collectives, backward(): summed, total = lax.psum((local_part, squares), 'rows')  42.4 us
    psum x1, blocking collectives, local(): lax.psum(jnp.sum(forward_rest * forward_rest, axis=1), 'rows')  21.4 us
    all_gather x1, waiting for transfers between devices, local(): lax.all_gather(sketch_piece, 'cols', axis=1, tiled=True)  17.1 us
    all_gather x2, blocking collectives, backward(): return (jnp.sqrt(total), lax.all_gather(summed, 'cols', axis=1, tiled=True))  11.1 us
  transfers between devices with their start and end apart: 6, of which 6 were waited for; matrix products, arithmetic and copies ran while one was open for 0% of the time, Pallas kernels for 0%

profile of v1, /device:TPU:0, one launch (start us, length us, event | category | flops | bytes accessed | tf_op | source)
XLA Modules:
  0.0 427.6 jit_solution(9721579525670645669)
XLA Ops:
  7.2 0.0 reduce-scatter.2.cloned.1.call-start
  7.3 0.7 compare_select_fusion.1
  8.0 0.7 compare_and_fusion.1
  8.8 6.2 %gather_fusion = bf16[2048,64]{1,0:T(8,128)(2,1)S(1)} fusion(bf16[64,64]{1,0:T(8,128)(2,1)S(1)} %select_convert_fusion, s32[2048]{0:T(1024)S(1)} %broadcast_clamp_fusion.1), kind=kCustom, calls=%fused_computation | custom fusion | bytes 532480 | tf_op jit(solution)/shard_map/jit(_take)/gather | solution.py:103
  14.9 0.0 copy-start.6
  15.0 0.3 broadcast_select_fusion.1
  15.3 0.2 copy.6
  15.6 6.2 %gather_fusion.1 = bf16[2048,32]{1,0:T(8,128)(2,1)S(1)} fusion(bf16[32,32]{1,0:T(8,128)(2,1)S(1)} %select_convert_fusion.1, s32[2048]{0:T(1024)S(1)} %broadcast_clamp_fusion), kind=kCustom, calls=%fused_computation.1 | custom fusion | bytes 270336 | tf_op jit(solution)/shard_map/jit(_take)/gather | solution.py:104
  21.7 0.3 broadcast_select_fusion
  22.1 0.2 copy.7
  22.3 0.0 copy-done.6
  22.3 0.0 copy-start.3
  22.3 0.6 broadcast_multiply_fusion
  22.9 0.7 copy-done.3
  23.5 4.2 convolution_multiply_fusion
  27.8 0.0 copy-start.4
  27.8 0.0 reduce-scatter.2.cloned.1.call-update
  27.8 0.0 all-gather.3.cloned.1.call-start
  27.8 71.2 %reduce-scatter.2.cloned.1.call-done = f32[256,256]{1,0:T(8,128)} async-done(((f32[2048,256]{1,0:T(8,128)}), f32[256,256]{1,0:T(8,128)}) %reduce-scatter.2.cloned.1.call-update) | async-done | bytes 262160 | tf_op jit(solution)/shard_map/reduce_scatter | solution.py:115
  99.0 0.0 all-gather.3.cloned.1.call-update
  99.1 0.0 all-reduce.6.cloned.1.call-start
  99.1 17.1 %all-gather.3.cloned.1.call-done = f32[256,1024]{1,0:T(8,128)} async-done(((f32[256,256]{1,0:T(8,128)}), f32[256,1024]{1,0:T(8,128)}) %all-gather.3.cloned.1.call-update) | async-done | bytes 1048592 | tf_op jit(solution)/shard_map/all_gather | solution.py:117
  116.2 4.1 fusion.20
  120.3 0.0 all-reduce.6.cloned.1.call-update
  120.3 0.0 all-gather.5.cloned.1.call-start
  120.3 78.3 %all-reduce.6.cloned.1.call-done = f32[1024,256]{1,0:T(8,128)} async-done(((f32[1024,256]{1,0:T(8,128)}), f32[1024,256]{1,0:T(8,128)}) %all-reduce.6.cloned.1.call-update) | async-done | bytes 1048592 | tf_op jit(solution)/shard_map/psum | solution.py:122
  198.6 0.0 all-gather.5.cloned.1.call-update
  198.6 0.0 all-reduce.8.cloned.1.call-start
  198.7 0.0 copy-done.4
  198.7 0.1 multiply_reduce_fusion.2
  198.8 0.5 fusion.19
  199.3 20.6 %all-reduce.1 = (f32[8,256]{1,0:T(8,128)S(1)}, f32[8]{0:T(128)S(1)}) all-reduce(f32[8,256]{1,0:T(8,128)S(1)} %fusion.19, f32[8]{0:T(128)S(1)} %multiply_reduce_fusion.2), channel_id=1, replica_groups=mesh['rows'=8,'cols'=4] {'rows'}, use_global_device_ids=true, to_apply=%region_0.1 | all-reduce | flops 2056 | bytes 16448 | tf_op jit(solution)/shard_map/psum | solution.py:136
  219.9 5.5 %all_gather.12 = f32[8,1024]{1,0:T(8,128)S(1)} all-gather(f32[8,256]{1,0:T(8,128)S(1)} %get-tuple-element.4), channel_id=1, replica_groups=mesh['rows'=8,'cols'=4] {'cols'}, dimensions={1}, use_global_device_ids=true | all-gather | bytes 40960 | tf_op jit(solution)/shard_map/all_gather | solution.py:137
  225.4 8.9 %all-gather.5.cloned.1.call-done.gram_ref = f32[1024,1024]{1,0:T(8,128)} async-done(((f32[1024,256]{1,0:T(8,128)}), f32[1024,1024]{1,0:T(8,128)}) %all-gather.5.cloned.1.call-update) | async-done | bytes 4194320 | tf_op jit(solution)/shard_map/all_gather | solution.py:123
  234.4 0.0 copy-start.2
  234.4 2.2 copy-done.2
  236.6 54.9 %shard_map.59 = f32[1024,1024]{1,0:T(8,128)S(1)} custom-call(f32[1024,1024]{1,0:T(8,128)S(1)} %copy-done.2), custom_call_target="tpu_custom_call" | custom-call | tf_op jit(solution)/shard_map/pallas_call | solution.py:89
  291.5 0.0 copy-start
  291.5 3.6 multiply_reduce_fusion.4
  295.2 2.1 fusion.15
  297.3 0.0 copy-done
  297.3 1.6 fusion.13
  298.8 0.0 all-reduce.8.cloned.1.call-update
  298.9 0.0 all-reduce.10.cloned.1.call-start
  298.9 31.1 %all-reduce.8.cloned.1.call-done = f32[8,2048]{1,0:T(8,128)} async-done(((f32[8,2048]{1,0:T(8,128)}), f32[8,2048]{1,0:T(8,128)}) %all-reduce.8.cloned.1.call-update) | async-done | bytes 65552 | tf_op jit(solution)/shard_map/psum | solution.py:131
  330.1 1.0 multiply_reduce_fusion.1
  331.1 0.5 fusion.21
  331.6 21.8 %all-reduce = (f32[8,256]{1,0:T(8,128)S(1)}, f32[8]{0:T(128)S(1)}) all-reduce(f32[8,256]{1,0:T(8,128)S(1)} %fusion.21, f32[8]{0:T(128)S(1)} %get-tuple-element.11), channel_id=1, replica_groups=mesh['rows'=8,'cols'=4] {'rows'}, use_global_device_ids=true, to_apply=%region_9.10 | all-reduce | flops 2056 | bytes 16448 | tf_op jit(solution)/shard_map/psum | solution.py:136
  353.5 0.0 copy-start.1
  353.5 5.5 %all_gather.15 = f32[8,1024]{1,0:T(8,128)S(1)} all-gather(f32[8,256]{1,0:T(8,128)S(1)} %get-tuple-element.2), channel_id=1, replica_groups=mesh['rows'=8,'cols'=4] {'cols'}, dimensions={1}, use_global_device_ids=true | all-gather | bytes 40960 | tf_op jit(solution)/shard_map/all_gather | solution.py:137
  359.0 0.0 copy-start.5
  359.0 5.8 %multiply_reduce_fusion.3 = (f32[8]{0:T(128)S(1)}, f32[8,1024]{1,0:T(8,128)S(1)}) fusion(f32[8,1024]{1,0:T(8,128)S(1)} %get-tuple-element.19, f32[8]{0:T(128)S(1)} %sqrt.30, f32[8]{0:T(128)S(1)} %sqrt.31, f32[1024,1024]{1,0:T(8,128)} %copy-done, f32[8,1024]{1,0:T(8,128)S(1)} %all_gather.15), kind=kOutput, calls=%fused_computation.18 | convolution fusion | flops 100712440 | bytes 4292704 | tf_op jit(solution)/shard_map/dot_general | solution.py:140
  364.9 0.0 copy-done.1
  364.9 2.1 fusion.2
  366.9 1.6 fusion.11
  368.5 0.0 all-reduce.10.cloned.1.call-update
  368.5 27.5 %all-reduce.10.cloned.1.call-done = f32[8,2048]{1,0:T(8,128)} async-done(((f32[8,2048]{1,0:T(8,128)}), f32[8,2048]{1,0:T(8,128)}) %all-reduce.10.cloned.1.call-update) | async-done | bytes 65552 | tf_op jit(solution)/shard_map/psum | solution.py:131
  396.0 1.0 multiply_reduce_fusion
  397.1 21.4 %psum.63 = f32[8]{0:T(128)S(1)} all-reduce(f32[8]{0:T(128)S(1)} %multiply_reduce_fusion), channel_id=1, replica_groups=mesh['rows'=8,'cols'=4] {'rows'}, use_global_device_ids=true, to_apply=%region_13.14 | all-reduce | flops 8 | bytes 64 | tf_op jit(solution)/shard_map/psum | solution.py:162
  418.5 0.7 multiply_add_fusion
  419.2 0.0 copy-done.5
  419.2 1.6 add_subtract_fusion
  (12 shorter events, 0.2 us)
Async XLA Ops:
  7.2 91.9 %reduce-scatter.2.cloned.1.call-start = ((), (), s32[]{:S(2)}) async-start(), calls=%async_computation.1 | async-start | bytes 2359296 | tf_op jit(solution)/shard_map/reduce_scatter | solution.py:115
  14.9 7.3 %copy-start.6 = (s32[2048]{0:T(1024)S(1)}, s32[2048]{0:T(1024)}, u32[]{:S(2)}) copy-start(s32[2048]{0:T(1024)} %param.5) | copy-start | bytes 24580
  22.3 1.2 copy-start.3
  27.8 170.9 %copy-start.4 = (f32[8,2048]{1,0:T(8,128)S(1)}, f32[8,2048]{1,0:T(8,128)}, u32[]{:S(2)}) copy-start(f32[8,2048]{1,0:T(8,128)} %param.7) | copy-start | bytes 196612
  27.8 88.4 %all-gather.3.cloned.1.call-start = ((), (), s32[]{:S(2)}) async-start(), calls=%async_computation.2 | async-start | bytes 1310720 | tf_op jit(solution)/shard_map/all_gather | solution.py:117
  99.1 99.5 %all-reduce.6.cloned.1.call-start = ((), (), s32[]{:S(2)}) async-start(), calls=%async_computation.3 | async-start | bytes 2097152 | tf_op jit(solution)/shard_map/psum | solution.py:122
  120.3 114.1 %all-gather.5.cloned.1.call-start = ((), (), s32[]{:S(2)}) async-start(), calls=%async_computation.4 | async-start | bytes 5242880 | tf_op jit(solution)/shard_map/all_gather | solution.py:123
  198.6 131.4 %all-reduce.8.cloned.1.call-start = ((), (), s32[]{:S(2)}) async-start(), calls=%async_computation.5 | async-start | bytes 131072 | tf_op jit(solution)/shard_map/psum | solution.py:131
  234.4 2.2 copy-start.2
  291.5 5.7 %copy-start = (f32[1024,1024]{1,0:T(8,128)}, f32[1024,1024]{1,0:T(8,128)S(1)}, u32[]{:S(2)}) copy-start(f32[1024,1024]{1,0:T(8,128)S(1)} %shard_map.59) | copy-start | bytes 12582916
  298.9 97.2 %all-reduce.10.cloned.1.call-start = ((), (), s32[]{:S(2)}) async-start(), calls=%async_computation.6 | async-start | bytes 131072 | tf_op jit(solution)/shard_map/psum | solution.py:131
  353.5 11.4 %copy-start.1 = (f32[1024,1024]{1,0:T(8,128)S(1)}, f32[1024,1024]{1,0:T(8,128)}, u32[]{:S(2)}) copy-start(f32[1024,1024]{1,0:T(8,128)} %copy-done) | copy-start | bytes 12582916
  359.0 60.1 %copy-start.5 = (f32[8,2048]{1,0:T(8,128)S(1)}, f32[8,2048]{1,0:T(8,128)}, u32[]{:S(2)}) copy-start(f32[8,2048]{1,0:T(8,128)} %all-reduce.8.cloned.1.call-done) | copy-start | bytes 196612
Sparse Core Ops, SparseCore 0:
  27.9 71.0 reduce-scatter.1
  100.6 15.5 all-gather.2
  120.4 78.1 all-reduce.5
  200.1 34.2 all-gather.4
  299.0 31.0 all-reduce.7
  368.7 27.3 all-reduce.9

commit v2 on v1

--- a/solution.py
+++ b/solution.py
@@ -96,6 +96,180 @@
     )(gram_matrix)
 
 
+MESH = pl.DeviceIdType.MESH
+
+
+def greet(axes):
+    barrier = pltpu.get_barrier_semaphore()
+    count = 0
+    for axis in axes:
+        size = lax.axis_size(axis)
+        me = lax.axis_index(axis)
+        for offset in range(1, size):
+            pl.semaphore_signal(
+                barrier, inc=1, device_id={axis: lax.rem(me + offset, size)}, device_id_type=MESH
+            )
+        count += size - 1
+    pl.semaphore_wait(barrier, count)
+
+
+def share(axis, value, slots, send_sem, recv_sem):
+    size = lax.axis_size(axis)
+    me = lax.axis_index(axis)
+    slots[me] = value
+
+    def copy(slot, offset, peer):
+        return pltpu.make_async_remote_copy(
+            src_ref=slots.at[slot], dst_ref=slots.at[slot],
+            send_sem=send_sem.at[offset - 1], recv_sem=recv_sem.at[slot],
+            device_id={axis: peer}, device_id_type=MESH,
+        )
+
+    for offset in range(1, size):
+        copy(me, offset, lax.rem(me + offset, size)).start()
+    for offset in range(1, size):
+        source = lax.rem(me + size - offset, size)
+        copy(source, offset, source).wait_recv()
+    for offset in range(1, size):
+        copy(me, offset, lax.rem(me + offset, size)).wait_send()
+
+
+def split_rows(vectors):
+    top = vectors.astype(jnp.bfloat16).astype(jnp.float32)
+    rest = vectors - top
+    middle = rest.astype(jnp.bfloat16).astype(jnp.float32)
+    low = rest - middle
+    return jnp.concatenate([top, middle, low, jnp.zeros_like(low)], axis=0).astype(jnp.bfloat16)
+
+
+def join_rows(stacked, systems):
+    return stacked[:systems] + stacked[systems:2 * systems] + stacked[2 * systems:3 * systems]
+
+
+def lsqr_kernel(
+    matrix_ref, inverse_ref, right_ref, solution_ref, residual_ref,
+    row_slots, col_slots, image_slots, norm_slots,
+    row_send, row_recv, col_send, col_recv, image_send, image_recv, norm_send, norm_recv,
+):
+    systems = right_ref.shape[0]
+    col_count = matrix_ref.shape[1]
+    own = pl.ds(pl.multiple_of(lax.axis_index("cols") * col_count, col_count), col_count)
+    greet(("rows", "cols"))
+
+    def added(slots):
+        total = slots[0]
+        for slot in range(1, slots.shape[0]):
+            total = total + slots[slot]
+        return total
+
+    def forward(own_part, turn):
+        product = lax.dot_general(
+            split_rows(own_part), matrix_ref[...], (((1,), (1,)), ((), ())),
+            preferred_element_type=jnp.float32,
+        )
+        share("cols", join_rows(product, systems), image_slots.at[turn], image_send.at[turn], image_recv.at[turn])
+        return added(image_slots.at[turn])
+
+    def backward(vectors, turn):
+        squares = jnp.sum(vectors * vectors, axis=1, keepdims=True)
+        product = jnp.dot(split_rows(vectors), matrix_ref[...], preferred_element_type=jnp.float32)
+        value = jnp.concatenate(
+            [join_rows(product, systems), jnp.broadcast_to(squares, (systems, col_count))], axis=0
+        )
+        share("rows", value, row_slots.at[turn], row_send.at[turn], row_recv.at[turn])
+        total = added(row_slots.at[turn])
+        norm = jnp.sqrt(total[systems:, 0:1])
+        share("cols", total[:systems] / norm, col_slots.at[turn], col_send.at[turn], col_recv.at[turn])
+        whole = jnp.concatenate([col_slots[turn, slot] for slot in range(col_slots.shape[1])], axis=1)
+        return norm, whole
+
+    def solve_right(vectors):
+        return lax.dot_general(
+            vectors, inverse_ref[...], (((1,), (1,)), ((), ())),
+            precision=highest, preferred_element_type=jnp.float32,
+        )
+
+    def solve_left(vectors):
+        return jnp.dot(vectors, inverse_ref[:, own], precision=highest, preferred_element_type=jnp.float32)
+
+    def norm_of(vectors):
+        return jnp.sqrt(jnp.sum(vectors * vectors, axis=1, keepdims=True))
+
+    right_sides = right_ref[...]
+    beta_norm, whole_vector = backward(right_sides, 0)
+    left_unit = right_sides / beta_norm
+    back_rest = solve_right(whole_vector)
+    alpha_norm = norm_of(back_rest)
+    right_unit = back_rest / alpha_norm
+    moved = solve_left(right_unit)
+    image = forward(moved, 0)
+    search, search_image = moved, image
+    coeffs = jnp.zeros_like(moved)
+    coeffs_image = jnp.zeros_like(image)
+    phibar = beta_norm
+    rhobar = alpha_norm
+    for iteration in range(ROUNDS):
+        last = iteration == ROUNDS - 1
+        forward_rest = image - alpha_norm * left_unit
+        if last:
+            squares = jnp.sum(forward_rest * forward_rest, axis=1, keepdims=True)
+            share("rows", jnp.broadcast_to(squares, norm_slots.shape[1:]), norm_slots, norm_send, norm_recv)
+            beta_norm = jnp.sqrt(added(norm_slots)[:, 0:1])
+        else:
+            beta_norm, whole_vector = backward(forward_rest, iteration + 1)
+        rho_total = jnp.sqrt(rhobar * rhobar + beta_norm * beta_norm)
+        cosine = rhobar / rho_total
+        sine_part = beta_norm / rho_total
+        ratio = cosine * phibar / rho_total
+        coeffs = coeffs + ratio * search
+        coeffs_image = coeffs_image + ratio * search_image
+        if last:
+            break
+        left_unit = forward_rest / beta_norm
+        back_rest = solve_right(whole_vector) - beta_norm * right_unit
+        alpha_norm = norm_of(back_rest)
+        right_unit = back_rest / alpha_norm
+        moved = solve_left(right_unit)
+        image = forward(moved, iteration + 1)
+        shrink = sine_part * alpha_norm / rho_total
+        rhobar = -cosine * alpha_norm
+        phibar = sine_part * phibar
+        search = moved - shrink * search
+        search_image = image - shrink * search_image
+    solution_ref[...] = coeffs
+    residual_ref[...] = right_sides - coeffs_image
+
+
+def lsqr(matrix, inverse, right_sides):
+    row_count, col_count = matrix.shape
+    systems = right_sides.shape[0]
+    row_size, col_size = lax.axis_size("rows"), lax.axis_size("cols")
+    vmem = pl.BlockSpec(memory_space=pltpu.VMEM)
+    dma = pltpu.SemaphoreType.DMA
+    return pl.pallas_call(
+        lsqr_kernel,
+        out_shape=(
+            jax.ShapeDtypeStruct((systems, col_count), jnp.float32),
+            jax.ShapeDtypeStruct((systems, row_count), jnp.float32),
+        ),
+        in_specs=[vmem] * 3,
+        out_specs=(vmem, vmem),
+        scratch_shapes=[
+            pltpu.VMEM((ROUNDS, row_size, 2 * systems, col_count), jnp.float32),
+            pltpu.VMEM((ROUNDS, col_size, systems, col_count), jnp.float32),
+            pltpu.VMEM((ROUNDS, col_size, systems, row_count), jnp.float32),
+            pltpu.VMEM((row_size, systems, 128), jnp.float32),
+            dma((ROUNDS, row_size)), dma((ROUNDS, row_size)),
+            dma((ROUNDS, col_size)), dma((ROUNDS, col_size)),
+            dma((ROUNDS, col_size)), dma((ROUNDS, col_size)),
+            dma((row_size,)), dma((row_size,)),
+        ],
+        compiler_params=pltpu.CompilerParams(
+            collective_id=0, has_side_effects=True, vmem_limit_bytes=40 * 1024 * 1024
+        ),
+    )(matrix, inverse, right_sides)
+
+
 def picked_mixer(sampled, row_count):
     bit_count = row_count.bit_length() - 1
     inner_order = 2 ** (bit_count // 2)
@@ -122,68 +296,7 @@
     gram_summed = lax.psum(gram_block, "rows")
     gram_matrix = lax.all_gather(gram_summed, "cols", axis=1, tiled=True)
     inverse = inverse_factor(gram_matrix)
-    col_start = lax.axis_index("cols") * col_count
-    wide = matrix.astype(jnp.float32)
-
-    def forward(vectors):
-        own_part = lax.dynamic_slice_in_dim(vectors, col_start, col_count, 1)
-        local_part = lax.dot_general(own_part, wide, (((1,), (1,)), ((), ())), precision=highest)
-        return lax.psum(local_part, "cols")
-
-    def backward(vectors):
-        squares = jnp.sum(vectors * vectors, axis=1)
-        local_part = jnp.dot(vectors, wide, precision=highest)
-        summed, total = lax.psum((local_part, squares), "rows")
-        return jnp.sqrt(total), lax.all_gather(summed, "cols", axis=1, tiled=True)
-
-    def solve_right(vectors):
-        return lax.dot_general(vectors, inverse, (((1,), (1,)), ((), ())), precision=highest)
-
-    def solve_left(vectors):
-        return jnp.dot(vectors, inverse, precision=highest)
-
-    beta_norm, whole_vector = backward(right_sides)
-    left_unit = right_sides / beta_norm[:, None]
-    back_rest = solve_right(whole_vector / beta_norm[:, None])
-    alpha_norm = jnp.sqrt(jnp.sum(back_rest * back_rest, axis=1))
-    right_unit = back_rest / alpha_norm[:, None]
-    moved = solve_left(right_unit)
-    image = forward(moved)
-    search, search_image = moved, image
-    full_solution = jnp.zeros_like(moved)
-    solution_image = jnp.zeros_like(image)
-    phibar = beta_norm
-    rhobar = alpha_norm
-    for iteration in range(ROUNDS):
-        forward_rest = image - alpha_norm[:, None] * left_unit
-        if iteration < ROUNDS - 1:
-            beta_norm, whole_vector = backward(forward_rest)
-        else:
-            beta_norm = jnp.sqrt(lax.psum(jnp.sum(forward_rest * forward_rest, axis=1), "rows"))
-        rho_total = jnp.sqrt(rhobar * rhobar + beta_norm * beta_norm)
-        cosine = rhobar / rho_total
-        sine_part = beta_norm / rho_total
-        phi_term = cosine * phibar
-        ratio = (phi_term / rho_total)[:, None]
-        full_solution = full_solution + ratio * search
-        solution_image = solution_image + ratio * search_image
-        if iteration == ROUNDS - 1:
-            break
-        left_unit = forward_rest / beta_norm[:, None]
-        back_rest = solve_right(whole_vector / beta_norm[:, None]) - beta_norm[:, None] * right_unit
-        alpha_norm = jnp.sqrt(jnp.sum(back_rest * back_rest, axis=1))
-        right_unit = back_rest / alpha_norm[:, None]
-        moved = solve_left(right_unit)
-        image = forward(moved)
-        theta_term = sine_part * alpha_norm
-        rhobar = -cosine * alpha_norm
-        phibar = sine_part * phibar
-        shrink = (theta_term / rho_total)[:, None]
-        search = moved - shrink * search
-        search_image = image - shrink * search_image
-    residual = right_sides - solution_image
-    solution = lax.dynamic_slice_in_dim(full_solution, col_start, col_count, 1)
-    return (solution, residual)
+    return lsqr(matrix, inverse, right_sides)
 
 
 def solution(mesh):

time: 428 us -> 343 us (0.80)
  blocking collectives: 74.8 us -> 0 us
  Pallas kernels: 54.9 us -> 99 us
  waiting for transfers between devices: 234 us -> 202 us
  matrix products: 26.1 us -> 8.26 us
    psum x3 -> x0, blocking collectives: 63.8 us -> none  [the longest x2 42.4 us: backward(): summed, total = lax.psum((local_part, squares), 'rows')]
    psum x2 -> x0, waiting for transfers between devices: 58.7 us -> none  [forward(): return lax.psum(local_part, 'cols')]
    pallas_call x0 -> x1, Pallas kernels: none -> 43.6 us  [lsqr(): pl.pallas_call(lsqr_kernel, out_shape=(jax.ShapeDtypeStruct((systems, col...]
    all_gather x1, waiting for transfers between devices: 8.94 us -> 35.6 us  [local(): gram_matrix = lax.all_gather(gram_summed, 'cols', axis=1, tiled=True)]
    dot_general x8 -> x0, matrix products: 17.8 us -> none  [the longest x2 9.44 us: solve_right(): lax.dot_general(vectors, inverse, (((1,), (1,)), ((), ())), precision=hig...]
    all_gather x2 -> x0, blocking collectives: 11.1 us -> none  [backward(): return (jnp.sqrt(total), lax.all_gather(summed, 'cols', axis=1, tiled=True))]
  transfers between devices with their start and end apart: 6 -> 4, of which waited for: 6 -> 4; matrix products, arithmetic and copies ran while one was open for 0% -> 0% of each run, Pallas kernels for 0% -> 0%
where the time goes in v2:
time: 343 us
  waiting for transfers between devices  202 us (59%)
  Pallas kernels  99 us (29%)
  local copies, waits for them, and re-layouts  16.2 us (5%)
  between operations  13.9 us (4%)
  matrix products  8.26 us (2%)
  other arithmetic  3.48 us (1%)
    psum x1, waiting for transfers between devices, local(): gram_summed = lax.psum(gram_block, 'rows')  78.2 us
    reduce_scatter x1, waiting for transfers between devices, local(): lax.psum_scatter(picked, 'rows', scatter_dimension=0, tiled=True)  70.6 us
    pallas_call x1, Pallas kernels, inverse_factor(): pl.pallas_call(inverse_factor_kernel, out_shape=jax.ShapeDtypeStruct((ord...  55.4 us
    pallas_call x1, Pallas kernels, lsqr(): pl.pallas_call(lsqr_kernel, out_shape=(jax.ShapeDtypeStruct((systems, col...  43.6 us
    all_gather x1, waiting for transfers between devices, local(): gram_matrix = lax.all_gather(gram_summed, 'cols', axis=1, tiled=True)  35.6 us
    all_gather x1, waiting for transfers between devices, local(): lax.all_gather(sketch_piece, 'cols', axis=1, tiled=True)  17.2 us
  transfers between devices with their start and end apart: 4, of which 4 were waited for; matrix products, arithmetic and copies ran while one was open for 0% of the time, Pallas kernels for 0%

profile of v2, /device:TPU:0, one launch (start us, length us, event | category | flops | bytes accessed | tf_op | source)
XLA Modules:
  0.0 342.7 jit_solution(5822405410893709231)
XLA Ops:
  7.2 0.0 reduce-scatter.2.cloned.1.call-start
  7.3 0.7 subtract_convert_fusion
  8.0 0.7 compare_select_fusion.1
  8.7 0.7 compare_and_fusion.1
  9.5 6.2 %gather_fusion = bf16[2048,64]{1,0:T(8,128)(2,1)S(1)} fusion(bf16[64,64]{1,0:T(8,128)(2,1)S(1)} %select_convert_fusion, s32[2048]{0:T(1024)S(1)} %broadcast_clamp_fusion.1), kind=kCustom, calls=%fused_computation | custom fusion | bytes 532480 | tf_op jit(solution)/shard_map/jit(_take)/gather | solution.py:277
  15.7 0.0 copy-start.1
  15.7 0.3 broadcast_select_fusion.1
  16.0 0.2 copy.6
  16.2 6.2 %gather_fusion.1 = bf16[2048,32]{1,0:T(8,128)(2,1)S(1)} fusion(bf16[32,32]{1,0:T(8,128)(2,1)S(1)} %select_convert_fusion.1, s32[2048]{0:T(1024)S(1)} %broadcast_clamp_fusion), kind=kCustom, calls=%fused_computation.1 | custom fusion | bytes 270336 | tf_op jit(solution)/shard_map/jit(_take)/gather | solution.py:278
  22.4 0.3 broadcast_select_fusion
  22.8 0.2 copy.7
  23.0 0.6 broadcast_multiply_fusion
  23.5 0.0 copy-done.1
  23.5 4.2 %convolution_multiply_fusion = f32[2048,256]{1,0:T(8,128)} fusion(bf16[2048,2048]{0,1:T(8,128)(2,1)S(1)} %bitcast.21, bf16[2048,256]{1,0:T(8,128)(2,1)S(1)} %copy-done.1, bf16[2048]{0:T(1024)(128)(2,1)S(1)} %subtract_convert_fusion), kind=kOutput, calls=%fused_computation.3 | convolution fusion | flops 2148532224 | bytes 11538432 | tf_op jit(solution)/shard_map/dot_general | solution.py:286
  27.7 0.0 copy-start.2
  27.8 0.0 reduce-scatter.2.cloned.1.call-update
  27.8 0.0 all-gather.3.cloned.1.call-start
  27.8 70.6 %reduce-scatter.2.cloned.1.call-done = f32[256,256]{1,0:T(8,128)} async-done(((f32[2048,256]{1,0:T(8,128)}), f32[256,256]{1,0:T(8,128)}) %reduce-scatter.2.cloned.1.call-update) | async-done | bytes 262160 | tf_op jit(solution)/shard_map/reduce_scatter | solution.py:289
  98.4 0.0 all-gather.3.cloned.1.call-update
  98.4 0.0 all-reduce.2.cloned.1.call-start
  98.5 17.2 %all-gather.3.cloned.1.call-done = f32[256,1024]{1,0:T(8,128)} async-done(((f32[256,256]{1,0:T(8,128)}), f32[256,1024]{1,0:T(8,128)}) %all-gather.3.cloned.1.call-update) | async-done | bytes 1048592 | tf_op jit(solution)/shard_map/all_gather | solution.py:291
  115.7 4.1 %fusion.4 = f32[1024,256]{1,0:T(8,128)} fusion(f32[256,1024]{1,0:T(8,128)} %all-gather.3.cloned.1.call-done, f32[256,256]{1,0:T(8,128)} %reduce-scatter.2.cloned.1.call-done), kind=kOutput, calls=%fused_computation.35 | convolution fusion | flops 805306368 | bytes 2359296 | tf_op jit(solution)/shard_map/dot_general | solution.py:290
  119.7 0.0 all-reduce.2.cloned.1.call-update
  119.8 0.0 all-gather.5.cloned.1.call-start
  119.8 78.2 %all-reduce.2.cloned.1.call-done = f32[1024,256]{1,0:T(8,128)} async-done(((f32[1024,256]{1,0:T(8,128)}), f32[1024,256]{1,0:T(8,128)}) %all-reduce.2.cloned.1.call-update) | async-done | bytes 1048592 | tf_op jit(solution)/shard_map/psum | solution.py:296
  198.1 0.0 all-gather.5.cloned.1.call-update
  198.1 35.6 %all-gather.5.cloned.1.call-done.gram_ref = f32[1024,1024]{1,0:T(8,128)} async-done(((f32[1024,256]{1,0:T(8,128)}), f32[1024,1024]{1,0:T(8,128)}) %all-gather.5.cloned.1.call-update) | async-done | bytes 4194320 | tf_op jit(solution)/shard_map/all_gather | solution.py:297
  233.7 0.0 copy-start
  233.7 2.2 copy-done
  235.9 55.4 %shard_map.59.inverse_ref = f32[1024,1024]{1,0:T(8,128)S(1)} custom-call(f32[1024,1024]{1,0:T(8,128)S(1)} %copy-done), custom_call_target="tpu_custom_call" | custom-call | tf_op jit(solution)/shard_map/pallas_call | solution.py:89
  291.3 0.0 copy-done.2
  291.3 43.6 %shard_map.60 = (f32[8,256]{1,0:T(8,128)S(1)}, f32[8,2048]{1,0:T(8,128)S(1)}) custom-call(bf16[2048,256]{1,0:T(8,128)(2,1)S(1)} %copy-done.1, f32[1024,1024]{1,0:T(8,128)S(1)} %shard_map.59.inverse_ref, f32[8,2048]{1,0:T(8,128)S(1)} %copy-done.2), custom_call_target="tpu_custom_call" | custom-call | tf_op jit(solution)/shard_map/pallas_call | solution.py:249
  334.9 0.6 copy.11
  335.5 0.6 copy.12
  (5 shorter events, 0.1 us)
Async XLA Ops:
  7.2 91.2 %reduce-scatter.2.cloned.1.call-start = ((), (), s32[]{:S(2)}) async-start(), calls=%async_computation.1 | async-start | bytes 2359296 | tf_op jit(solution)/shard_map/reduce_scatter | solution.py:289
  15.7 7.8 %copy-start.1 = (bf16[2048,256]{1,0:T(8,128)(2,1)S(1)}, bf16[2048,256]{1,0:T(8,128)(2,1)}, u32[]{:S(2)}) copy-start(bf16[2048,256]{1,0:T(8,128)(2,1)} %matrix_ref.1) | copy-start | bytes 3145732
  27.7 263.5 %copy-start.2 = (f32[8,2048]{1,0:T(8,128)S(1)}, f32[8,2048]{1,0:T(8,128)}, u32[]{:S(2)}) copy-start(f32[8,2048]{1,0:T(8,128)} %right_ref.1) | copy-start | bytes 196612
  27.8 87.9 %all-gather.3.cloned.1.call-start = ((), (), s32[]{:S(2)}) async-start(), calls=%async_computation.2 | async-start | bytes 1310720 | tf_op jit(solution)/shard_map/all_gather | solution.py:291
  98.4 99.6 %all-reduce.2.cloned.1.call-start = ((), (), s32[]{:S(2)}) async-start(), calls=%async_computation.3 | async-start | bytes 2097152 | tf_op jit(solution)/shard_map/psum | solution.py:296
  119.8 113.9 %all-gather.5.cloned.1.call-start = ((), (), s32[]{:S(2)}) async-start(), calls=%async_computation.4 | async-start | bytes 5242880 | tf_op jit(solution)/shard_map/all_gather | solution.py:297
  233.7 2.2 copy-start
Sparse Core Ops, SparseCore 0:
  27.9 70.4 reduce-scatter.1
  100.0 15.6 all-gather.2
  119.9 78.1 all-reduce.1
  199.6 34.0 all-gather.4

commit v3 on v2

--- a/solution.py
+++ b/solution.py
@@ -13,15 +13,6 @@
 STRIP = 8
 
 highest = lax.Precision.HIGHEST
-
-
-def sylvester(matrix_order):
-    positions = jnp.arange(matrix_order, dtype=jnp.int32)
-    common = jnp.bitwise_and(positions[:, None], positions[None, :])
-    parity = jnp.zeros((matrix_order, matrix_order), jnp.int32)
-    for bit_place in range(max(matrix_order.bit_length() - 1, 0)):
-        parity = parity + jnp.bitwise_and(jnp.right_shift(common, bit_place), 1)
-    return jnp.where(jnp.bitwise_and(parity, 1) == 0, 1.0, -1.0).astype(jnp.float32)
 
 
 def block_inverse(square):
@@ -54,9 +45,11 @@
 
 
 def inverse_factor_kernel(gram_ref, out_ref, strip_ref):
-    order = gram_ref.shape[0]
+    order = gram_ref.shape[1]
     blocks = order // BLOCK
-    out_ref[...] = gram_ref[...]
+    width = gram_ref.shape[2]
+    for col_block in range(gram_ref.shape[0]):
+        out_ref[:, col_block * width:(col_block + 1) * width] = gram_ref[col_block]
 
     def step(block, carry):
         start = pl.multiple_of(block * BLOCK, BLOCK)
@@ -85,7 +78,7 @@
 
 
 def inverse_factor(gram_matrix):
-    order = gram_matrix.shape[0]
+    order = gram_matrix.shape[1]
     return pl.pallas_call(
         inverse_factor_kernel,
         out_shape=jax.ShapeDtypeStruct((order, order), jnp.float32),
@@ -113,25 +106,50 @@
     pl.semaphore_wait(barrier, count)
 
 
-def share(axis, value, slots, send_sem, recv_sem):
+def share_copy(axis, slots, send_sem, recv_sem, offset, incoming):
     size = lax.axis_size(axis)
     me = lax.axis_index(axis)
-    slots[me] = value
-
-    def copy(slot, offset, peer):
-        return pltpu.make_async_remote_copy(
-            src_ref=slots.at[slot], dst_ref=slots.at[slot],
-            send_sem=send_sem.at[offset - 1], recv_sem=recv_sem.at[slot],
-            device_id={axis: peer}, device_id_type=MESH,
-        )
-
-    for offset in range(1, size):
-        copy(me, offset, lax.rem(me + offset, size)).start()
-    for offset in range(1, size):
-        source = lax.rem(me + size - offset, size)
-        copy(source, offset, source).wait_recv()
-    for offset in range(1, size):
-        copy(me, offset, lax.rem(me + offset, size)).wait_send()
+    peer = lax.rem(me + (size - offset if incoming else offset), size)
+    slot = peer if incoming else me
+    return pltpu.make_async_remote_copy(
+        src_ref=slots.at[slot], dst_ref=slots.at[slot],
+        send_sem=send_sem.at[offset - 1], recv_sem=recv_sem.at[slot],
+        device_id={axis: peer}, device_id_type=MESH,
+    )
+
+
+def share_start(axis, value, slots, send_sem, recv_sem):
+    slots[lax.axis_index(axis)] = value
+    for offset in range(1, lax.axis_size(axis)):
+        share_copy(axis, slots, send_sem, recv_sem, offset, False).start()
+
+
+def share_finish(axis, slots, send_sem, recv_sem):
+    for offset in range(1, lax.axis_size(axis)):
+        share_copy(axis, slots, send_sem, recv_sem, offset, True).wait_recv()
+    for offset in range(1, lax.axis_size(axis)):
+        share_copy(axis, slots, send_sem, recv_sem, offset, False).wait_send()
+
+
+def share(axis, value, slots, send_sem, recv_sem):
+    share_start(axis, value, slots, send_sem, recv_sem)
+    share_finish(axis, slots, send_sem, recv_sem)
+
+
+def added(slots):
+    total = slots[0]
+    for slot in range(1, slots.shape[0]):
+        total = total + slots[slot]
+    return total
+
+
+def backward_part(vectors, matrix_ref):
+    systems = vectors.shape[0]
+    squares = jnp.sum(vectors * vectors, axis=1, keepdims=True)
+    product = jnp.dot(split_rows(vectors), matrix_ref[...], preferred_element_type=jnp.float32)
+    return jnp.concatenate(
+        [join_rows(product, systems), jnp.broadcast_to(squares, (systems, matrix_ref.shape[1]))], axis=0
+    )
 
 
 def split_rows(vectors):
@@ -147,7 +165,7 @@
 
 
 def lsqr_kernel(
-    matrix_ref, inverse_ref, right_ref, solution_ref, residual_ref,
+    matrix_ref, inverse_ref, right_ref, first_ref, norm_ref, solution_ref, residual_ref,
     row_slots, col_slots, image_slots, norm_slots,
     row_send, row_recv, col_send, col_recv, image_send, image_recv, norm_send, norm_recv,
 ):
@@ -156,12 +174,6 @@
     own = pl.ds(pl.multiple_of(lax.axis_index("cols") * col_count, col_count), col_count)
     greet(("rows", "cols"))
 
-    def added(slots):
-        total = slots[0]
-        for slot in range(1, slots.shape[0]):
-            total = total + slots[slot]
-        return total
-
     def forward(own_part, turn):
         product = lax.dot_general(
             split_rows(own_part), matrix_ref[...], (((1,), (1,)), ((), ())),
@@ -171,12 +183,7 @@
         return added(image_slots.at[turn])
 
     def backward(vectors, turn):
-        squares = jnp.sum(vectors * vectors, axis=1, keepdims=True)
-        product = jnp.dot(split_rows(vectors), matrix_ref[...], preferred_element_type=jnp.float32)
-        value = jnp.concatenate(
-            [join_rows(product, systems), jnp.broadcast_to(squares, (systems, col_count))], axis=0
-        )
-        share("rows", value, row_slots.at[turn], row_send.at[turn], row_recv.at[turn])
+        share("rows", backward_part(vectors, matrix_ref), row_slots.at[turn], row_send.at[turn], row_recv.at[turn])
         total = added(row_slots.at[turn])
         norm = jnp.sqrt(total[systems:, 0:1])
         share("cols", total[:systems] / norm, col_slots.at[turn], col_send.at[turn], col_recv.at[turn])
@@ -196,7 +203,8 @@
         return jnp.sqrt(jnp.sum(vectors * vectors, axis=1, keepdims=True))
 
     right_sides = right_ref[...]
-    beta_norm, whole_vector = backward(right_sides, 0)
+    beta_norm = norm_ref[:, 0:1]
+    whole_vector = jnp.concatenate([first_ref[slot] for slot in range(first_ref.shape[0])], axis=1)
     left_unit = right_sides / beta_norm
     back_rest = solve_right(whole_vector)
     alpha_norm = norm_of(back_rest)
@@ -216,7 +224,7 @@
             share("rows", jnp.broadcast_to(squares, norm_slots.shape[1:]), norm_slots, norm_send, norm_recv)
             beta_norm = jnp.sqrt(added(norm_slots)[:, 0:1])
         else:
-            beta_norm, whole_vector = backward(forward_rest, iteration + 1)
+            beta_norm, whole_vector = backward(forward_rest, iteration)
         rho_total = jnp.sqrt(rhobar * rhobar + beta_norm * beta_norm)
         cosine = rhobar / rho_total
         sine_part = beta_norm / rho_total
@@ -240,7 +248,7 @@
     residual_ref[...] = right_sides - coeffs_image
 
 
-def lsqr(matrix, inverse, right_sides):
+def lsqr(matrix, inverse, right_sides, first, norm):
     row_count, col_count = matrix.shape
     systems = right_sides.shape[0]
     row_size, col_size = lax.axis_size("rows"), lax.axis_size("cols")
@@ -252,51 +260,257 @@
             jax.ShapeDtypeStruct((systems, col_count), jnp.float32),
             jax.ShapeDtypeStruct((systems, row_count), jnp.float32),
         ),
-        in_specs=[vmem] * 3,
+        in_specs=[vmem] * 5,
         out_specs=(vmem, vmem),
         scratch_shapes=[
-            pltpu.VMEM((ROUNDS, row_size, 2 * systems, col_count), jnp.float32),
-            pltpu.VMEM((ROUNDS, col_size, systems, col_count), jnp.float32),
+            pltpu.VMEM((ROUNDS - 1, row_size, 2 * systems, col_count), jnp.float32),
+            pltpu.VMEM((ROUNDS - 1, col_size, systems, col_count), jnp.float32),
             pltpu.VMEM((ROUNDS, col_size, systems, row_count), jnp.float32),
             pltpu.VMEM((row_size, systems, 128), jnp.float32),
-            dma((ROUNDS, row_size)), dma((ROUNDS, row_size)),
-            dma((ROUNDS, col_size)), dma((ROUNDS, col_size)),
+            dma((ROUNDS - 1, row_size)), dma((ROUNDS - 1, row_size)),
+            dma((ROUNDS - 1, col_size)), dma((ROUNDS - 1, col_size)),
             dma((ROUNDS, col_size)), dma((ROUNDS, col_size)),
             dma((row_size,)), dma((row_size,)),
         ],
         compiler_params=pltpu.CompilerParams(
             collective_id=0, has_side_effects=True, vmem_limit_bytes=40 * 1024 * 1024
         ),
-    )(matrix, inverse, right_sides)
+    )(matrix, inverse, right_sides, first, norm)
 
 
 def picked_mixer(sampled, row_count):
-    bit_count = row_count.bit_length() - 1
-    inner_order = 2 ** (bit_count // 2)
-    outer_order = row_count // inner_order
-    outer = jnp.take(sylvester(outer_order).astype(jnp.bfloat16), sampled // inner_order, axis=0)
-    inner = jnp.take(sylvester(inner_order).astype(jnp.bfloat16), sampled % inner_order, axis=0)
-    return (outer[:, :, None] * inner[:, None, :]).reshape(sampled.shape[0], row_count)
+    count = sampled.shape[0]
+    lanes = min(128, row_count)
+    common = sampled & lax.broadcasted_iota(jnp.int32, (count, lanes), 1)
+    for shift in (4, 2, 1):
+        common = common ^ lax.shift_right_logical(common, shift)
+    mixer = jnp.where((common & 1) == 0, 1.0, -1.0).astype(jnp.float32)
+    width = lanes
+    while width < row_count:
+        sign = jnp.where((sampled & width) == 0, 1.0, -1.0).astype(jnp.float32)
+        mixer = jnp.concatenate([mixer, mixer * sign], axis=1)
+        width = 2 * width
+    return mixer.astype(jnp.bfloat16)
+
+
+def col_bits(size):
+    return [1 << place for place in range(size.bit_length() - 2, -1, -1)]
+
+
+def gram_kernel(
+    signed_ref, sampled_ref, matrix_ref, right_ref, gram_ref, first_ref, norm_ref,
+    sketch_out, sketch_near, sketch_sum, sketch_far, pieces, partial,
+    gram_out, gram_near, gram_sum, gram_far, row_slots,
+    near_send, near_recv, far_send, far_recv, piece_send, piece_recv,
+    block_send, block_recv, block_far_send, row_send, row_recv, col_send, col_recv,
+):
+    row_size, col_size = lax.axis_size("rows"), lax.axis_size("cols")
+    row, col = lax.axis_index("rows"), lax.axis_index("cols")
+    inner_size = 2 if row_size % 2 == 0 else 1
+    outer_size = row_size // inner_size
+    inner, outer = lax.rem(row, inner_size), row // inner_size
+    row_count, col_count = signed_ref.shape
+    sketch_rows = sampled_ref.shape[0]
+    systems = right_ref.shape[0]
+    bits = col_bits(col_size)
+    started = []
+
+    def flip(place, bit):
+        return place + bit - 2 * bit * lax.rem(place // bit, 2)
+
+    def start(source, target, send_sem, recv_sem, device):
+        copy = pltpu.make_async_remote_copy(
+            src_ref=source, dst_ref=target, send_sem=send_sem, recv_sem=recv_sem,
+            device_id=device, device_id_type=MESH,
+        )
+        copy.start()
+        started.append(copy)
+
+    def arrived(target, recv_sem, device):
+        pltpu.make_async_remote_copy(
+            src_ref=target, dst_ref=target, send_sem=recv_sem, recv_sem=recv_sem,
+            device_id=device, device_id_type=MESH,
+        ).wait_recv()
+
+    near_peer = {"rows": outer * inner_size + (inner_size - 1 - inner)}
+    outer_order = [lax.rem(outer + step, outer_size) for step in range(1, outer_size)] + [outer]
+
+    def reduce_scatter(turn, chunk, out, near, summed, far):
+        if inner_size == 2:
+            for other in outer_order:
+                out[other] = chunk(other * inner_size + 1 - inner)
+                start(out.at[other], near.at[other], near_send.at[turn, other], near_recv.at[turn, other], near_peer)
+        total = None
+        for step, other in enumerate(outer_order):
+            total = chunk(other * inner_size + inner)
+            if inner_size == 2:
+                arrived(near.at[other], near_recv.at[turn, other], near_peer)
+                total = total + near[other]
+            if step < outer_size - 1:
+                summed[other] = total
+                start(
+                    summed.at[other], far.at[outer], far_send.at[turn, other], far_recv.at[turn, outer],
+                    {"rows": other * inner_size + inner},
+                )
+        for offset in range(1, outer_size):
+            source = lax.rem(outer + outer_size - offset, outer_size)
+            arrived(far.at[source], far_recv.at[turn, source], {"rows": source * inner_size + inner})
+            total = total + far[source]
+        return total
+
+    greet(("rows", "cols"))
+
+    share_start("rows", backward_part(right_ref[...], matrix_ref), row_slots, row_send, row_recv)
+
+    piece_rows = sketch_rows // row_size
+
+    def sketch_chunk(target):
+        sampled = sampled_ref[pl.ds(pl.multiple_of(target * piece_rows, piece_rows), piece_rows), :]
+        return jnp.dot(
+            picked_mixer(sampled, row_count), signed_ref[...], preferred_element_type=jnp.float32
+        ) * (1.0 / math.sqrt(sketch_rows))
+
+    own_piece = reduce_scatter(0, sketch_chunk, sketch_out, sketch_near, sketch_sum, sketch_far)
+    pieces[col] = own_piece
+    for place, bit in enumerate(bits):
+        start(pieces.at[col], pieces.at[col], piece_send.at[place, col], piece_recv.at[col], {"cols": flip(col, bit)})
+
+    share_finish("rows", row_slots, row_send, row_recv)
+    first_total = added(row_slots)
+    first_norm = jnp.sqrt(first_total[systems:])
+    norm_ref[...] = first_norm[:, :norm_ref.shape[1]]
+    share_start("cols", first_total[:systems] / first_norm, first_ref, col_send, col_recv)
+
+    masks = sorted(range(1, col_size), key=lambda mask: (-(mask & -mask), mask))
+
+    def other_col(mask):
+        place = col
+        for bit in bits:
+            if mask & bit:
+                place = flip(place, bit)
+        return place
+
+    def multiply(block):
+        partial[pl.ds(pl.multiple_of(block * col_count, col_count), col_count), :] = lax.dot_general(
+            pieces[block], pieces[col], (((0,), (0,)), ((), ())),
+            precision=highest, preferred_element_type=jnp.float32,
+        )
+
+    multiply(col)
+    for mask in masks:
+        block = other_col(mask)
+        arrived(pieces.at[block], piece_recv.at[block], {"cols": flip(col, mask & -mask)})
+        for place, bit in enumerate(bits):
+            if bit < (mask & -mask):
+                start(
+                    pieces.at[block], pieces.at[block], piece_send.at[place, block], piece_recv.at[block],
+                    {"cols": flip(col, bit)},
+                )
+        multiply(block)
+
+    block_rows = gram_ref.shape[1] // row_size
+
+    def rows_of(target):
+        return pl.ds(pl.multiple_of(target * block_rows, block_rows), block_rows)
+
+    total = reduce_scatter(
+        1, lambda target: partial[rows_of(target), :], gram_out, gram_near, gram_sum, gram_far
+    )
+
+    def block_ref(block_row, block_col):
+        return gram_ref.at[block_col, rows_of(block_row), :]
+
+    def pass_on(block_row, block_col, below):
+        for place, bit in enumerate(bits):
+            if bit < below:
+                start(
+                    block_ref(block_row, block_col), block_ref(block_row, block_col),
+                    block_send.at[place, block_row, block_col], block_recv.at[block_row, block_col],
+                    {"cols": flip(col, bit)},
+                )
+
+    def pass_near(block_row):
+        if inner_size == 2:
+            start(
+                block_ref(block_row, col), block_ref(block_row, col),
+                block_send.at[len(bits), block_row, col], block_recv.at[block_row, col], near_peer,
+            )
+
+    gram_ref[col, rows_of(row), :] = total
+    for offset in range(1, outer_size):
+        other = lax.rem(outer + offset, outer_size)
+        start(
+            block_ref(row, col), block_ref(row, col), block_far_send.at[offset], block_recv.at[row, col],
+            {"rows": other * inner_size + inner},
+        )
+    pass_near(row)
+    pass_on(row, col, col_size)
+    for offset in range(1, outer_size):
+        source = lax.rem(outer + outer_size - offset, outer_size) * inner_size + inner
+        arrived(block_ref(source, col), block_recv.at[source, col], {"rows": source})
+        pass_near(source)
+        pass_on(source, col, col_size)
+    by_distance = [lax.rem(outer + outer_size - offset, outer_size) for offset in range(outer_size)]
+    if inner_size == 2:
+        for other in by_distance:
+            source = other * inner_size + 1 - inner
+            arrived(block_ref(source, col), block_recv.at[source, col], near_peer)
+            pass_on(source, col, col_size)
+    for mask in masks:
+        block = other_col(mask)
+        for layer in range(inner_size):
+            for other in by_distance:
+                source = other * inner_size + (inner if layer == 0 else 1 - inner)
+                arrived(block_ref(source, block), block_recv.at[source, block], {"cols": flip(col, mask & -mask)})
+                pass_on(source, block, mask & -mask)
+    share_finish("cols", first_ref, col_send, col_recv)
+    for copy in started:
+        copy.wait_send()
+
+
+def sketched_gram(signed, sampled, matrix, right_sides):
+    row_count, col_count = matrix.shape
+    systems = right_sides.shape[0]
+    sketch_rows = sampled.shape[0]
+    row_size, col_size = lax.axis_size("rows"), lax.axis_size("cols")
+    inner_size = 2 if row_size % 2 == 0 else 1
+    outer_size = row_size // inner_size
+    order = col_count * col_size
+    bit_total = max(len(col_bits(col_size)), 1)
+    vmem = pl.BlockSpec(memory_space=pltpu.VMEM)
+    dma = pltpu.SemaphoreType.DMA
+    float_vmem = lambda *shape: pltpu.VMEM(shape, jnp.float32)
+    return pl.pallas_call(
+        gram_kernel,
+        out_shape=(
+            jax.ShapeDtypeStruct((col_size, order, col_count), jnp.float32),
+            jax.ShapeDtypeStruct((col_size, systems, col_count), jnp.float32),
+            jax.ShapeDtypeStruct((systems, 128), jnp.float32),
+        ),
+        in_specs=[vmem] * 4,
+        out_specs=(vmem, vmem, vmem),
+        scratch_shapes=[float_vmem(outer_size, sketch_rows // row_size, col_count)] * 4
+        + [float_vmem(col_size, sketch_rows // row_size, col_count), float_vmem(order, col_count)]
+        + [float_vmem(outer_size, order // row_size, col_count)] * 4
+        + [
+            float_vmem(row_size, 2 * systems, col_count),
+            dma((2, outer_size)), dma((2, outer_size)), dma((2, outer_size)), dma((2, outer_size)),
+            dma((bit_total, col_size)), dma((col_size,)),
+            dma((bit_total + 1, row_size, col_size)), dma((row_size, col_size)), dma((outer_size,)),
+            dma((row_size,)), dma((row_size,)), dma((col_size,)), dma((col_size,)),
+        ],
+        compiler_params=pltpu.CompilerParams(
+            collective_id=1, has_side_effects=True, vmem_limit_bytes=48 * 1024 * 1024
+        ),
+    )(signed, sampled, matrix, right_sides)
 
 
 def local(matrix, row_signs, sampled_rows, right_sides):
-    row_count, col_count = matrix.shape
-    flipped = (1 - 2 * row_signs).astype(jnp.bfloat16)
-    signed = matrix * flipped[:, None]
-    picked = jnp.dot(
-        picked_mixer(sampled_rows[0], row_count), signed, preferred_element_type=jnp.float32
-    ) * (1.0 / math.sqrt(sampled_rows.shape[1]))
-    sketch_piece = lax.psum_scatter(picked, "rows", scatter_dimension=0, tiled=True)
-    gram_block = lax.dot_general(
-        lax.all_gather(sketch_piece, "cols", axis=1, tiled=True),
-        sketch_piece,
-        (((0,), (0,)), ((), ())),
-        precision=highest,
-    )
-    gram_summed = lax.psum(gram_block, "rows")
-    gram_matrix = lax.all_gather(gram_summed, "cols", axis=1, tiled=True)
+    signed = matrix * (1 - 2 * row_signs).astype(jnp.bfloat16)[:, None]
+    sampled = sampled_rows.reshape(-1, 1)
+    gram_matrix, first, norm = sketched_gram(signed, sampled, matrix, right_sides)
     inverse = inverse_factor(gram_matrix)
-    return lsqr(matrix, inverse, right_sides)
+    return lsqr(matrix, inverse, right_sides, first, norm)
 
 
 def solution(mesh):

time: 343 us -> 201 us (0.59)
  waiting for transfers between devices: 202 us -> 0 us
  Pallas kernels: 99 us -> 191 us
  between operations: 13.9 us -> 0.69 us
  local copies, waits for them, and re-layouts: 16.2 us -> 6.53 us
  matrix products: 8.26 us -> 0 us
    pallas_call x0 -> x1, Pallas kernels: none -> 96.6 us  [sketched_gram(): pl.pallas_call(gram_kernel, out_shape=(jax.ShapeDtypeStruct((col_size, or...]
    psum x1 -> x0, waiting for transfers between devices: 78.2 us -> none  [local(): gram_summed = lax.psum(gram_block, 'rows')]
    reduce_scatter x1 -> x0, waiting for transfers between devices: 70.6 us -> none  [local(): lax.psum_scatter(picked, 'rows', scatter_dimension=0, tiled=True)]
    all_gather x2 -> x0, waiting for transfers between devices: 52.8 us -> none  [the longest x1 35.6 us: local(): gram_matrix = lax.all_gather(gram_summed, 'cols', axis=1, tiled=True)]
    gather x2 -> x0, local copies, waits for them, and re-layouts: 12.4 us -> none  [the longest x1 6.18 us: picked_mixer(): jnp.take(sylvester(outer_order).astype(jnp.bfloat16), sampled // inner_or...]
    dot_general x2 -> x0, matrix products: 8.26 us -> none  [the longest x1 4.21 us: local(): jnp.dot(picked_mixer(sampled_rows[0], row_count), signed, preferred_eleme...]
    pallas_call x1, Pallas kernels: 43.6 us -> 38.9 us  [lsqr(): pl.pallas_call(lsqr_kernel, out_shape=(jax.ShapeDtypeStruct((systems, col...]
  transfers between devices with their start and end apart: 4 -> 0, of which waited for: 4 -> 0; matrix products, arithmetic and copies ran while one was open for 0% -> 0% of each run, Pallas kernels for 0% -> 0%
where the time goes in v3:
time: 201 us; the launch traced here: 200 us
  Pallas kernels  191 us (95%)
  local copies, waits for them, and re-layouts  6.53 us (3%)
  other arithmetic  2.26 us (1%)
    pallas_call x1, Pallas kernels, sketched_gram(): pl.pallas_call(gram_kernel, out_shape=(jax.ShapeDtypeStruct((col_size, or...  96.6 us
    pallas_call x1, Pallas kernels, inverse_factor(): pl.pallas_call(inverse_factor_kernel, out_shape=jax.ShapeDtypeStruct((ord...  55.4 us
    pallas_call x1, Pallas kernels, lsqr(): pl.pallas_call(lsqr_kernel, out_shape=(jax.ShapeDtypeStruct((systems, col...  38.9 us
    unnamed x8, local copies, waits for them, and re-layouts  5.47 us

profile of v3, /device:TPU:0, one launch (start us, length us, event | category | flops | bytes accessed | tf_op | source)
XLA Modules:
  0.0 200.3 jit_solution(8690839498126853869)
XLA Ops:
  0.6 0.7 subtract_convert_fusion
  1.3 1.6 broadcast_multiply_fusion.signed_ref
  2.9 1.1 copy.6.sampled_ref
  4.0 0.0 copy-start
  4.0 1.2 copy-done
  5.2 0.0 copy-start.2
  5.2 0.8 copy-done.2
  6.0 96.6 %shard_map.59 = (f32[4,1024,256]{2,1,0:T(8,128)}, f32[4,8,256]{2,1,0:T(8,128)S(1)}, f32[8,128]{1,0:T(8,128)S(1)}) custom-call(bf16[2048,256]{1,0:T(8,128)(2,1)S(1)} %broadcast_multiply_fusion.signed_ref, s32[2048,1]{1,0:T(8,128)S(1)} %copy.6.sampled_ref, bf16[2048,256]{1,0:T(8,128)(2,1)S(1)} %copy-done, f32[8,2048]{1,0:T(8,128)S(1)} %copy-done.2), custom_call_target="tpu_custom_call" | custom-call | tf_op jit(solution)/shard_map/pallas_call | solution.py:483
  102.6 0.0 copy-start.1
  102.6 2.2 %copy-done.1 = f32[4,1024,256]{2,1,0:T(8,128)S(1)} copy-done((f32[4,1024,256]{2,1,0:T(8,128)S(1)}, f32[4,1024,256]{2,1,0:T(8,128)}, u32[]{:S(2)}) %copy-start.1) | copy-done | bytes 4194328
  104.8 55.4 %shard_map.60.inverse_ref = f32[1024,1024]{1,0:T(8,128)S(1)} custom-call(f32[4,1024,256]{2,1,0:T(8,128)S(1)} %copy-done.1), custom_call_target="tpu_custom_call" | custom-call | tf_op jit(solution)/shard_map/pallas_call | solution.py:82
  160.2 38.9 %shard_map.61 = (f32[8,256]{1,0:T(8,128)S(1)}, f32[8,2048]{1,0:T(8,128)S(1)}) custom-call(bf16[2048,256]{1,0:T(8,128)(2,1)S(1)} %copy-done, f32[1024,1024]{1,0:T(8,128)S(1)} %shard_map.60.inverse_ref, f32[8,2048]{1,0:T(8,128)S(1)} %copy-done.2, f32[4,8,256]{2,1,0:T(8,128)S(1)} %get-tuple-element.6.first_ref, f32[8,128]{1,0:T(8,128)S(1)} %get-tuple-element.7.norm_ref), custom_call_target="tpu_custom_call" | custom-call | tf_op jit(solution)/shard_map/pallas_call | solution.py:257
  199.1 0.6 copy.9
  199.7 0.6 copy.10
Async XLA Ops:
  4.0 1.2 copy-start
  5.2 0.8 copy-start.2
  102.6 2.2 %copy-start.1 = (f32[4,1024,256]{2,1,0:T(8,128)S(1)}, f32[4,1024,256]{2,1,0:T(8,128)}, u32[]{:S(2)}) copy-start(f32[4,1024,256]{2,1,0:T(8,128)} %get-tuple-element.5.gram_ref) | copy-start | bytes 12582916

commit v4 on v3

--- a/solution.py
+++ b/solution.py
@@ -45,11 +45,23 @@
 
 
 def inverse_factor_kernel(gram_ref, out_ref, strip_ref):
-    order = gram_ref.shape[1]
+    order = out_ref.shape[0]
     blocks = order // BLOCK
-    width = gram_ref.shape[2]
-    for col_block in range(gram_ref.shape[0]):
-        out_ref[:, col_block * width:(col_block + 1) * width] = gram_ref[col_block]
+    col_size, _, width = gram_ref.shape
+    half = width // 2
+    for col in range(col_size):
+        for other in range(col_size):
+            low, high = min(col, other), max(col, other)
+            start = low * width + (half if col > other else 0)
+            if col == other:
+                out_ref[start:start + width, high * width:(high + 1) * width] = gram_ref[col, :width, :]
+                continue
+            place = width + half * ((col ^ other) - 1)
+            out_ref[start:start + half, high * width:(high + 1) * width] = gram_ref[col, place:place + half, :]
+            if col > other:
+                out_ref[col * width:(col + 1) * width, other * width:(other + 1) * width] = jnp.zeros(
+                    (width, width), jnp.float32
+                )
 
     def step(block, carry):
         start = pl.multiple_of(block * BLOCK, BLOCK)
@@ -78,7 +90,7 @@
 
 
 def inverse_factor(gram_matrix):
-    order = gram_matrix.shape[1]
+    order = gram_matrix.shape[0] * gram_matrix.shape[2]
     return pl.pallas_call(
         inverse_factor_kernel,
         out_shape=jax.ShapeDtypeStruct((order, order), jnp.float32),
@@ -278,7 +290,8 @@
     )(matrix, inverse, right_sides, first, norm)
 
 
-def picked_mixer(sampled, row_count):
+def picked_mixer(sampled, signs):
+    row_count = signs.shape[1]
     count = sampled.shape[0]
     lanes = min(128, row_count)
     common = sampled & lax.broadcasted_iota(jnp.int32, (count, lanes), 1)
@@ -290,7 +303,7 @@
         sign = jnp.where((sampled & width) == 0, 1.0, -1.0).astype(jnp.float32)
         mixer = jnp.concatenate([mixer, mixer * sign], axis=1)
         width = 2 * width
-    return mixer.astype(jnp.bfloat16)
+    return (mixer * signs).astype(jnp.bfloat16)
 
 
 def col_bits(size):
@@ -298,7 +311,7 @@
 
 
 def gram_kernel(
-    signed_ref, sampled_ref, matrix_ref, right_ref, gram_ref, first_ref, norm_ref,
+    signs_ref, sampled_ref, matrix_ref, right_ref, gram_ref, first_ref, norm_ref,
     sketch_out, sketch_near, sketch_sum, sketch_far, pieces, partial,
     gram_out, gram_near, gram_sum, gram_far, row_slots,
     near_send, near_recv, far_send, far_recv, piece_send, piece_recv,
@@ -309,7 +322,7 @@
     inner_size = 2 if row_size % 2 == 0 else 1
     outer_size = row_size // inner_size
     inner, outer = lax.rem(row, inner_size), row // inner_size
-    row_count, col_count = signed_ref.shape
+    col_count = matrix_ref.shape[1]
     sketch_rows = sampled_ref.shape[0]
     systems = right_ref.shape[0]
     bits = col_bits(col_size)
@@ -364,10 +377,12 @@
 
     piece_rows = sketch_rows // row_size
 
+    signs = (1 - 2 * signs_ref[...]).astype(jnp.float32)
+
     def sketch_chunk(target):
         sampled = sampled_ref[pl.ds(pl.multiple_of(target * piece_rows, piece_rows), piece_rows), :]
         return jnp.dot(
-            picked_mixer(sampled, row_count), signed_ref[...], preferred_element_type=jnp.float32
+            picked_mixer(sampled, signs), matrix_ref[...], preferred_element_type=jnp.float32
         ) * (1.0 / math.sqrt(sketch_rows))
 
     own_piece = reduce_scatter(0, sketch_chunk, sketch_out, sketch_near, sketch_sum, sketch_far)
@@ -390,13 +405,27 @@
                 place = flip(place, bit)
         return place
 
-    def multiply(block):
-        partial[pl.ds(pl.multiple_of(block * col_count, col_count), col_count), :] = lax.dot_general(
-            pieces[block], pieces[col], (((0,), (0,)), ((), ())),
-            precision=highest, preferred_element_type=jnp.float32,
-        )
-
-    multiply(col)
+    half = col_count // 2
+
+    def product(left, right):
+        return lax.dot_general(
+            left, right, (((0,), (0,)), ((), ())), precision=highest, preferred_element_type=jnp.float32
+        )
+
+    def multiply(mask, block):
+        top = 1 << (mask.bit_length() - 1)
+        upper = lax.rem(col // top, 2)
+        low = col - upper * (col - block)
+        high = col + block - low
+        place = col_count + half * (mask - 1)
+        partial[place:place + half, :] = product(
+            pieces[low, :, pl.ds(pl.multiple_of(upper * half, half), half)], pieces[high]
+        )
+
+    partial[:col_count, :] = product(own_piece, own_piece)
+    used = col_count + half * (col_size - 1)
+    if used < partial.shape[0]:
+        partial[used:, :] = jnp.zeros((partial.shape[0] - used, col_count), jnp.float32)
     for mask in masks:
         block = other_col(mask)
         arrived(pieces.at[block], piece_recv.at[block], {"cols": flip(col, mask & -mask)})
@@ -406,7 +435,7 @@
                     pieces.at[block], pieces.at[block], piece_send.at[place, block], piece_recv.at[block],
                     {"cols": flip(col, bit)},
                 )
-        multiply(block)
+        multiply(mask, block)
 
     block_rows = gram_ref.shape[1] // row_size
 
@@ -468,14 +497,15 @@
         copy.wait_send()
 
 
-def sketched_gram(signed, sampled, matrix, right_sides):
+def sketched_gram(row_signs, sampled, matrix, right_sides):
     row_count, col_count = matrix.shape
     systems = right_sides.shape[0]
     sketch_rows = sampled.shape[0]
     row_size, col_size = lax.axis_size("rows"), lax.axis_size("cols")
     inner_size = 2 if row_size % 2 == 0 else 1
     outer_size = row_size // inner_size
-    order = col_count * col_size
+    used = col_count + col_count // 2 * (col_size - 1)
+    stack = row_size * STRIP * pl.cdiv(used, row_size * STRIP)
     bit_total = max(len(col_bits(col_size)), 1)
     vmem = pl.BlockSpec(memory_space=pltpu.VMEM)
     dma = pltpu.SemaphoreType.DMA
@@ -483,15 +513,15 @@
     return pl.pallas_call(
         gram_kernel,
         out_shape=(
-            jax.ShapeDtypeStruct((col_size, order, col_count), jnp.float32),
+            jax.ShapeDtypeStruct((col_size, stack, col_count), jnp.float32),
             jax.ShapeDtypeStruct((col_size, systems, col_count), jnp.float32),
             jax.ShapeDtypeStruct((systems, 128), jnp.float32),
         ),
         in_specs=[vmem] * 4,
         out_specs=(vmem, vmem, vmem),
         scratch_shapes=[float_vmem(outer_size, sketch_rows // row_size, col_count)] * 4
-        + [float_vmem(col_size, sketch_rows // row_size, col_count), float_vmem(order, col_count)]
-        + [float_vmem(outer_size, order // row_size, col_count)] * 4
+        + [float_vmem(col_size, sketch_rows // row_size, col_count), float_vmem(stack, col_count)]
+        + [float_vmem(outer_size, stack // row_size, col_count)] * 4
         + [
             float_vmem(row_size, 2 * systems, col_count),
             dma((2, outer_size)), dma((2, outer_size)), dma((2, outer_size)), dma((2, outer_size)),
@@ -502,13 +532,12 @@
         compiler_params=pltpu.CompilerParams(
             collective_id=1, has_side_effects=True, vmem_limit_bytes=48 * 1024 * 1024
         ),
-    )(signed, sampled, matrix, right_sides)
+    )(row_signs, sampled, matrix, right_sides)
 
 
 def local(matrix, row_signs, sampled_rows, right_sides):
-    signed = matrix * (1 - 2 * row_signs).astype(jnp.bfloat16)[:, None]
     sampled = sampled_rows.reshape(-1, 1)
-    gram_matrix, first, norm = sketched_gram(signed, sampled, matrix, right_sides)
+    gram_matrix, first, norm = sketched_gram(row_signs.reshape(1, -1), sampled, matrix, right_sides)
     inverse = inverse_factor(gram_matrix)
     return lsqr(matrix, inverse, right_sides, first, norm)
 

time: 201 us -> 179 us (0.89)
  Pallas kernels: 191 us -> 173 us
  other arithmetic: 2.26 us -> 0 us
    pallas_call x1, Pallas kernels: 96.6 us -> 81.7 us  [sketched_gram(): pl.pallas_call(gram_kernel, out_shape=(jax.ShapeDtypeStruct((col_size, st...]
    pallas_call x1, Pallas kernels: 38.9 us -> 36.1 us  [lsqr(): pl.pallas_call(lsqr_kernel, out_shape=(jax.ShapeDtypeStruct((systems, col...]
where the time goes in v4:
time: 179 us
  Pallas kernels  173 us (97%)
  local copies, waits for them, and re-layouts  5.04 us (3%)
    pallas_call x1, Pallas kernels, sketched_gram(): pl.pallas_call(gram_kernel, out_shape=(jax.ShapeDtypeStruct((col_size, st...  81.7 us
    pallas_call x1, Pallas kernels, inverse_factor(): pl.pallas_call(inverse_factor_kernel, out_shape=jax.ShapeDtypeStruct((ord...  55.3 us
    pallas_call x1, Pallas kernels, lsqr(): pl.pallas_call(lsqr_kernel, out_shape=(jax.ShapeDtypeStruct((systems, col...  36.1 us
    unnamed x8, local copies, waits for them, and re-layouts  3.99 us

profile of v4, /device:TPU:0, one launch (start us, length us, event | category | flops | bytes accessed | tf_op | source)
XLA Modules:
  0.0 178.9 jit_solution(10392872452660850022)
XLA Ops:
  0.6 1.1 copy.6.sampled_ref
  1.7 0.0 copy-start
  1.7 1.2 copy-done
  2.9 0.0 copy-start.1
  2.9 0.8 copy-done.1
  3.8 0.0 copy-start.2
  3.8 0.7 copy-done.2
  4.5 81.7 %shard_map.59 = (f32[4,640,256]{2,1,0:T(8,128)S(1)}, f32[4,8,256]{2,1,0:T(8,128)S(1)}, f32[8,128]{1,0:T(8,128)S(1)}) custom-call(s32[1,2048]{1,0:T(1,128)S(1)} %bitcast.2, s32[2048,1]{1,0:T(8,128)S(1)} %copy.6.sampled_ref, bf16[2048,256]{1,0:T(8,128)(2,1)S(1)} %copy-done, f32[8,2048]{1,0:T(8,128)S(1)} %copy-done.1), custom_call_target="tpu_custom_call" | custom-call | tf_op jit(solution)/shard_map/pallas_call | solution.py:513
  86.2 55.3 %shard_map.60.inverse_ref = f32[1024,1024]{1,0:T(8,128)S(1)} custom-call(f32[4,640,256]{2,1,0:T(8,128)S(1)} %get-tuple-element.5.gram_ref), custom_call_target="tpu_custom_call" | custom-call | tf_op jit(solution)/shard_map/pallas_call | solution.py:94
  141.5 36.1 %shard_map.61 = (f32[8,256]{1,0:T(8,128)S(1)}, f32[8,2048]{1,0:T(8,128)S(1)}) custom-call(bf16[2048,256]{1,0:T(8,128)(2,1)S(1)} %copy-done, f32[1024,1024]{1,0:T(8,128)S(1)} %shard_map.60.inverse_ref, f32[8,2048]{1,0:T(8,128)S(1)} %copy-done.1, f32[4,8,256]{2,1,0:T(8,128)S(1)} %get-tuple-element.6.first_ref, f32[8,128]{1,0:T(8,128)S(1)} %get-tuple-element.7.norm_ref), custom_call_target="tpu_custom_call" | custom-call | tf_op jit(solution)/shard_map/pallas_call | solution.py:269
  177.6 0.6 copy.9
  178.2 0.6 copy.10
Async XLA Ops:
  1.7 1.2 copy-start
  2.9 0.8 copy-start.1
  3.8 0.7 copy-start.2

commit v5 on v4

--- a/solution.py
+++ b/solution.py
@@ -15,7 +15,7 @@
 highest = lax.Precision.HIGHEST
 
 
-def block_inverse(square):
+def block_inverse(square, beside):
     size = square.shape[0]
     row_ids = lax.broadcasted_iota(jnp.int32, (size, size), 0)
     col_ids = lax.broadcasted_iota(jnp.int32, (size, size), 1)
@@ -23,6 +23,7 @@
     unit = jnp.where(row_ids == col_ids, 1.0, 0.0).astype(jnp.float32)
     finished = []
     for strip in range(size // STRIP):
+        beside(strip)
         start = strip * STRIP
         height = size - start
         here = lax.broadcasted_iota(jnp.int32, (height, size), 0)
@@ -44,8 +45,15 @@
     return jnp.concatenate(finished, axis=0)
 
 
-def inverse_factor_kernel(gram_ref, out_ref, strip_ref):
-    order = out_ref.shape[0]
+def three_parts(values):
+    top = values.astype(jnp.bfloat16)
+    rest = values - top.astype(jnp.float32)
+    middle = rest.astype(jnp.bfloat16)
+    return top, middle, (rest - middle.astype(jnp.float32)).astype(jnp.bfloat16)
+
+
+def inverse_factor_kernel(gram_ref, out_ref, left_ref, right_ref):
+    order = out_ref.shape[1]
     blocks = order // BLOCK
     col_size, _, width = gram_ref.shape
     half = width // 2
@@ -63,27 +71,37 @@
                     (width, width), jnp.float32
                 )
 
+    out_ref[order:, :] = jnp.zeros((BLOCK, order), jnp.float32)
+    left_ref[...] = jnp.zeros(left_ref.shape, jnp.bfloat16)
+    right_ref[...] = jnp.zeros(right_ref.shape, jnp.bfloat16)
+    col_ids = lax.broadcasted_iota(jnp.int32, (BLOCK, order), 1)
+
     def step(block, carry):
         start = pl.multiple_of(block * BLOCK, BLOCK)
         own = pl.ds(start, BLOCK)
-        inverse = block_inverse(out_ref[own, own])
-        strip_ref[...] = jnp.dot(
+        square = out_ref[own, own] - jnp.dot(
+            left_ref[own, :], right_ref[:, own], preferred_element_type=jnp.float32
+        )
+
+        def update(strip):
+            strips = BLOCK // STRIP
+            for slot in range(strip * (blocks - 1) // strips, (strip + 1) * (blocks - 1) // strips):
+                rows = pl.ds(pl.multiple_of(jnp.minimum(block + slot, blocks) * BLOCK, BLOCK), BLOCK)
+                reduction = jnp.dot(left_ref[rows, :], right_ref[...], preferred_element_type=jnp.float32)
+                fresh = (col_ids >= start - BLOCK) & (col_ids < start)
+                out_ref[rows, :] = jnp.where(fresh, 0.0, out_ref[rows, :]) - reduction
+
+        inverse = block_inverse(square, update)
+        rows_done = jnp.dot(
             inverse, out_ref[own, :], precision=highest, preferred_element_type=jnp.float32
         )
-        strip_ref[:, own] = inverse
-
-        def update(row_block, inner):
-            rows = pl.ds(pl.multiple_of(row_block * BLOCK, BLOCK), BLOCK)
-            out_ref[rows, own] = jnp.zeros((BLOCK, BLOCK), jnp.float32)
-            out_ref[rows, :] = out_ref[rows, :] - lax.dot_general(
-                strip_ref[:, rows], strip_ref[...], (((0,), (0,)), ((), ())),
-                precision=highest, preferred_element_type=jnp.float32,
-            )
-            return inner
-
-        lax.fori_loop(block + 1, blocks, update, 0)
-        col_ids = lax.broadcasted_iota(jnp.int32, (BLOCK, order), 1)
-        out_ref[own, :] = jnp.where(col_ids < start + BLOCK, strip_ref[...], 0.0)
+        wide_inverse = jnp.concatenate([inverse] * blocks, axis=1)
+        rows_done = jnp.where((col_ids >= start) & (col_ids < start + BLOCK), wide_inverse, rows_done)
+        top, middle, low = three_parts(rows_done)
+        right_ref[...] = jnp.concatenate([top, middle, top, middle, low, top], axis=0)
+        top, middle, low = three_parts(rows_done.T)
+        left_ref[:order, :] = jnp.concatenate([top, top, middle, middle, top, low], axis=1)
+        out_ref[own, :] = jnp.where(col_ids < start + BLOCK, rows_done, 0.0)
         return carry
 
     lax.fori_loop(0, blocks, step, 0)
@@ -93,10 +111,13 @@
     order = gram_matrix.shape[0] * gram_matrix.shape[2]
     return pl.pallas_call(
         inverse_factor_kernel,
-        out_shape=jax.ShapeDtypeStruct((order, order), jnp.float32),
+        out_shape=jax.ShapeDtypeStruct((order + BLOCK, order), jnp.float32),
         in_specs=[pl.BlockSpec(memory_space=pltpu.VMEM)],
         out_specs=pl.BlockSpec(memory_space=pltpu.VMEM),
-        scratch_shapes=[pltpu.VMEM((BLOCK, order), jnp.float32)],
+        scratch_shapes=[
+            pltpu.VMEM((order + BLOCK, 6 * BLOCK), jnp.bfloat16),
+            pltpu.VMEM((6 * BLOCK, order), jnp.bfloat16),
+        ],
         compiler_params=pltpu.CompilerParams(vmem_limit_bytes=32 * 1024 * 1024),
     )(gram_matrix)
 
@@ -183,6 +204,7 @@
 ):
     systems = right_ref.shape[0]
     col_count = matrix_ref.shape[1]
+    order = inverse_ref.shape[1]
     own = pl.ds(pl.multiple_of(lax.axis_index("cols") * col_count, col_count), col_count)
     greet(("rows", "cols"))
 
@@ -204,12 +226,12 @@
 
     def solve_right(vectors):
         return lax.dot_general(
-            vectors, inverse_ref[...], (((1,), (1,)), ((), ())),
+            vectors, inverse_ref[:order, :], (((1,), (1,)), ((), ())),
             precision=highest, preferred_element_type=jnp.float32,
         )
 
     def solve_left(vectors):
-        return jnp.dot(vectors, inverse_ref[:, own], precision=highest, preferred_element_type=jnp.float32)
+        return jnp.dot(vectors, inverse_ref[:order, own], precision=highest, preferred_element_type=jnp.float32)
 
     def norm_of(vectors):
         return jnp.sqrt(jnp.sum(vectors * vectors, axis=1, keepdims=True))

time: 179 us -> 170 us (0.950)
  Pallas kernels: 173 us -> 164 us
    pallas_call x1, Pallas kernels: 55.3 us -> 45.9 us  [inverse_factor(): pl.pallas_call(inverse_factor_kernel, out_shape=jax.ShapeDtypeStruct((ord...]
where the time goes in v5:
time: 170 us; the launch traced here: 169 us
  Pallas kernels  164 us (96%)
  local copies, waits for them, and re-layouts  5.04 us (3%)
    pallas_call x1, Pallas kernels, sketched_gram(): pl.pallas_call(gram_kernel, out_shape=(jax.ShapeDtypeStruct((col_size, st...  81.7 us
    pallas_call x1, Pallas kernels, inverse_factor(): pl.pallas_call(inverse_factor_kernel, out_shape=jax.ShapeDtypeStruct((ord...  45.9 us
    pallas_call x1, Pallas kernels, lsqr(): pl.pallas_call(lsqr_kernel, out_shape=(jax.ShapeDtypeStruct((systems, col...  36.1 us
    unnamed x8, local copies, waits for them, and re-layouts  3.99 us

profile of v5, /device:TPU:0, one launch (start us, length us, event | category | flops | bytes accessed | tf_op | source)
XLA Modules:
  0.0 169.5 jit_solution(8500556080117737463)
XLA Ops:
  0.6 1.1 copy.6.sampled_ref
  1.7 0.0 copy-start
  1.7 1.2 copy-done
  2.9 0.0 copy-start.1
  2.9 0.8 copy-done.1
  3.8 0.0 copy-start.2
  3.8 0.7 copy-done.2
  4.5 81.7 %shard_map.59 = (f32[4,640,256]{2,1,0:T(8,128)S(1)}, f32[4,8,256]{2,1,0:T(8,128)S(1)}, f32[8,128]{1,0:T(8,128)S(1)}) custom-call(s32[1,2048]{1,0:T(1,128)S(1)} %bitcast.2, s32[2048,1]{1,0:T(8,128)S(1)} %copy.6.sampled_ref, bf16[2048,256]{1,0:T(8,128)(2,1)S(1)} %copy-done, f32[8,2048]{1,0:T(8,128)S(1)} %copy-done.1), custom_call_target="tpu_custom_call" | custom-call | tf_op jit(solution)/shard_map/pallas_call | solution.py:535
  86.2 45.9 %shard_map.60.inverse_ref = f32[1152,1024]{1,0:T(8,128)S(1)} custom-call(f32[4,640,256]{2,1,0:T(8,128)S(1)} %get-tuple-element.5.gram_ref), custom_call_target="tpu_custom_call" | custom-call | tf_op jit(solution)/shard_map/pallas_call | solution.py:112
  132.1 36.1 %shard_map.61 = (f32[8,256]{1,0:T(8,128)S(1)}, f32[8,2048]{1,0:T(8,128)S(1)}) custom-call(bf16[2048,256]{1,0:T(8,128)(2,1)S(1)} %copy-done, f32[1152,1024]{1,0:T(8,128)S(1)} %shard_map.60.inverse_ref, f32[8,2048]{1,0:T(8,128)S(1)} %copy-done.1, f32[4,8,256]{2,1,0:T(8,128)S(1)} %get-tuple-element.6.first_ref, f32[8,128]{1,0:T(8,128)S(1)} %get-tuple-element.7.norm_ref), custom_call_target="tpu_custom_call" | custom-call | tf_op jit(solution)/shard_map/pallas_call | solution.py:291
  168.3 0.6 copy.9
  168.9 0.6 copy.10
Async XLA Ops:
  1.7 1.2 copy-start
  2.9 0.8 copy-start.1
  3.8 0.7 copy-start.2

commit v6 on v5

--- a/solution.py
+++ b/solution.py
@@ -52,7 +52,7 @@
     return top, middle, (rest - middle.astype(jnp.float32)).astype(jnp.bfloat16)
 
 
-def inverse_factor_kernel(gram_ref, out_ref, left_ref, right_ref):
+def inverse_factor_kernel(gram_ref, out_ref, inverse_ref, left_ref, right_ref):
     order = out_ref.shape[1]
     blocks = order // BLOCK
     col_size, _, width = gram_ref.shape
@@ -72,39 +72,50 @@
                 )
 
     out_ref[order:, :] = jnp.zeros((BLOCK, order), jnp.float32)
-    left_ref[...] = jnp.zeros(left_ref.shape, jnp.bfloat16)
-    right_ref[...] = jnp.zeros(right_ref.shape, jnp.bfloat16)
+    left_ref[order:, :] = jnp.zeros((BLOCK, left_ref.shape[1]), jnp.bfloat16)
+    inverse_ref[...] = jnp.zeros((BLOCK, BLOCK), jnp.float32)
     col_ids = lax.broadcasted_iota(jnp.int32, (BLOCK, order), 1)
+
+    def times(left, right, contract):
+        return lax.dot_general(
+            left, right, (((contract,), (0,)), ((), ())), precision=highest, preferred_element_type=jnp.float32
+        )
+
+    def finish(rows, start):
+        inverse = inverse_ref[...]
+        done = times(inverse, out_ref[rows, :], 1)
+        fresh = (col_ids >= start) & (col_ids < start + BLOCK)
+        done = jnp.where(fresh, jnp.concatenate([inverse] * blocks, axis=1), done)
+        out_ref[rows, :] = jnp.where(col_ids < start + BLOCK, done, 0.0)
+        return done
 
     def step(block, carry):
         start = pl.multiple_of(block * BLOCK, BLOCK)
         own = pl.ds(start, BLOCK)
-        square = out_ref[own, own] - jnp.dot(
-            left_ref[own, :], right_ref[:, own], preferred_element_type=jnp.float32
-        )
-
-        def update(strip):
+        before = pl.ds(pl.multiple_of(lax.rem(block + blocks, blocks + 1) * BLOCK, BLOCK), BLOCK)
+        strip_part = times(inverse_ref[...], out_ref[before, own], 1)
+        square = out_ref[own, own] - times(strip_part, strip_part, 0)
+
+        def beside(strip):
             strips = BLOCK // STRIP
+            if strip == 0:
+                done = finish(before, start - BLOCK)
+                top, middle, low = three_parts(done)
+                right_ref[...] = jnp.concatenate([top, middle, top, middle, low, top], axis=0)
+                top, middle, low = three_parts(done.T)
+                left_ref[:order, :] = jnp.concatenate([top, top, middle, middle, top, low], axis=1)
             for slot in range(strip * (blocks - 1) // strips, (strip + 1) * (blocks - 1) // strips):
                 rows = pl.ds(pl.multiple_of(jnp.minimum(block + slot, blocks) * BLOCK, BLOCK), BLOCK)
                 reduction = jnp.dot(left_ref[rows, :], right_ref[...], preferred_element_type=jnp.float32)
                 fresh = (col_ids >= start - BLOCK) & (col_ids < start)
                 out_ref[rows, :] = jnp.where(fresh, 0.0, out_ref[rows, :]) - reduction
 
-        inverse = block_inverse(square, update)
-        rows_done = jnp.dot(
-            inverse, out_ref[own, :], precision=highest, preferred_element_type=jnp.float32
-        )
-        wide_inverse = jnp.concatenate([inverse] * blocks, axis=1)
-        rows_done = jnp.where((col_ids >= start) & (col_ids < start + BLOCK), wide_inverse, rows_done)
-        top, middle, low = three_parts(rows_done)
-        right_ref[...] = jnp.concatenate([top, middle, top, middle, low, top], axis=0)
-        top, middle, low = three_parts(rows_done.T)
-        left_ref[:order, :] = jnp.concatenate([top, top, middle, middle, top, low], axis=1)
-        out_ref[own, :] = jnp.where(col_ids < start + BLOCK, rows_done, 0.0)
+        inverse = block_inverse(square, beside)
+        inverse_ref[...] = inverse
         return carry
 
     lax.fori_loop(0, blocks, step, 0)
+    finish(pl.ds(order - BLOCK, BLOCK), order - BLOCK)
 
 
 def inverse_factor(gram_matrix):
@@ -115,6 +126,7 @@
         in_specs=[pl.BlockSpec(memory_space=pltpu.VMEM)],
         out_specs=pl.BlockSpec(memory_space=pltpu.VMEM),
         scratch_shapes=[
+            pltpu.VMEM((BLOCK, BLOCK), jnp.float32),
             pltpu.VMEM((order + BLOCK, 6 * BLOCK), jnp.bfloat16),
             pltpu.VMEM((6 * BLOCK, order), jnp.bfloat16),
         ],
@@ -314,16 +326,17 @@
 
 def picked_mixer(sampled, signs):
     row_count = signs.shape[1]
-    count = sampled.shape[0]
+    count = sampled.shape[1]
     lanes = min(128, row_count)
-    common = sampled & lax.broadcasted_iota(jnp.int32, (count, lanes), 1)
+    wide = jnp.broadcast_to(sampled, (lanes, count)).T
+    common = wide & lax.broadcasted_iota(jnp.int32, (count, lanes), 1)
     for shift in (4, 2, 1):
         common = common ^ lax.shift_right_logical(common, shift)
     mixer = jnp.where((common & 1) == 0, 1.0, -1.0).astype(jnp.float32)
     width = lanes
     while width < row_count:
-        sign = jnp.where((sampled & width) == 0, 1.0, -1.0).astype(jnp.float32)
-        mixer = jnp.concatenate([mixer, mixer * sign], axis=1)
+        sign = jnp.where((wide & width) == 0, 1.0, -1.0).astype(jnp.float32)
+        mixer = jnp.concatenate([mixer, mixer * jnp.concatenate([sign] * (width // lanes), axis=1)], axis=1)
         width = 2 * width
     return (mixer * signs).astype(jnp.bfloat16)
 
@@ -345,7 +358,7 @@
     outer_size = row_size // inner_size
     inner, outer = lax.rem(row, inner_size), row // inner_size
     col_count = matrix_ref.shape[1]
-    sketch_rows = sampled_ref.shape[0]
+    sketch_rows = sampled_ref.shape[0] * sampled_ref.shape[1]
     systems = right_ref.shape[0]
     bits = col_bits(col_size)
     started = []
@@ -397,12 +410,10 @@
 
     share_start("rows", backward_part(right_ref[...], matrix_ref), row_slots, row_send, row_recv)
 
-    piece_rows = sketch_rows // row_size
-
     signs = (1 - 2 * signs_ref[...]).astype(jnp.float32)
 
     def sketch_chunk(target):
-        sampled = sampled_ref[pl.ds(pl.multiple_of(target * piece_rows, piece_rows), piece_rows), :]
+        sampled = sampled_ref[pl.ds(target, 1), :]
         return jnp.dot(
             picked_mixer(sampled, signs), matrix_ref[...], preferred_element_type=jnp.float32
         ) * (1.0 / math.sqrt(sketch_rows))
@@ -522,7 +533,7 @@
 def sketched_gram(row_signs, sampled, matrix, right_sides):
     row_count, col_count = matrix.shape
     systems = right_sides.shape[0]
-    sketch_rows = sampled.shape[0]
+    sketch_rows = sampled.shape[0] * sampled.shape[1]
     row_size, col_size = lax.axis_size("rows"), lax.axis_size("cols")
     inner_size = 2 if row_size % 2 == 0 else 1
     outer_size = row_size // inner_size
@@ -558,7 +569,7 @@
 
 
 def local(matrix, row_signs, sampled_rows, right_sides):
-    sampled = sampled_rows.reshape(-1, 1)
+    sampled = sampled_rows.reshape(lax.axis_size("rows"), -1)
     gram_matrix, first, norm = sketched_gram(row_signs.reshape(1, -1), sampled, matrix, right_sides)
     inverse = inverse_factor(gram_matrix)
     return lsqr(matrix, inverse, right_sides, first, norm)

time: 170 us -> 165 us (0.971)
  Pallas kernels: 164 us -> 159 us
    pallas_call x1, Pallas kernels: 45.9 us -> 40.7 us  [inverse_factor(): pl.pallas_call(inverse_factor_kernel, out_shape=jax.ShapeDtypeStruct((ord...]
    unnamed x8 -> x9, local copies, waits for them, and re-layouts: 3.99 us -> 4.5 us
where the time goes in v6:
time: 165 us
  Pallas kernels  159 us (96%)
  local copies, waits for them, and re-layouts  4.5 us (3%)
    pallas_call x1, Pallas kernels, sketched_gram(): pl.pallas_call(gram_kernel, out_shape=(jax.ShapeDtypeStruct((col_size, st...  81.7 us
    pallas_call x1, Pallas kernels, inverse_factor(): pl.pallas_call(inverse_factor_kernel, out_shape=jax.ShapeDtypeStruct((ord...  40.7 us
    pallas_call x1, Pallas kernels, lsqr(): pl.pallas_call(lsqr_kernel, out_shape=(jax.ShapeDtypeStruct((systems, col...  36.1 us
    unnamed x9, local copies, waits for them, and re-layouts  4.5 us

profile of v6, /device:TPU:0, one launch (start us, length us, event | category | flops | bytes accessed | tf_op | source)
XLA Modules:
  0.0 165.1 jit_solution(514917686664357089)
XLA Ops:
  0.6 0.5 broadcast.3
  1.1 1.4 reduce.3
  2.5 0.0 copy-start
  2.5 1.2 copy-done
  3.7 0.0 copy-start.1
  3.8 0.8 copy-done.1
  4.6 0.0 copy-start.2
  4.6 0.7 copy-done.2
  5.3 81.7 %shard_map.59 = (f32[4,640,256]{2,1,0:T(8,128)S(1)}, f32[4,8,256]{2,1,0:T(8,128)S(1)}, f32[8,128]{1,0:T(8,128)S(1)}) custom-call(s32[1,2048]{1,0:T(1,128)S(1)} %bitcast.1, s32[8,256]{1,0:T(8,128)S(1)} %reshape.11.sampled_ref, bf16[2048,256]{1,0:T(8,128)(2,1)S(1)} %copy-done, f32[8,2048]{1,0:T(8,128)S(1)} %copy-done.1), custom_call_target="tpu_custom_call" | custom-call | tf_op jit(solution)/shard_map/pallas_call | solution.py:546
  87.0 40.7 %shard_map.60.inverse_ref = f32[1152,1024]{1,0:T(8,128)S(1)} custom-call(f32[4,640,256]{2,1,0:T(8,128)S(1)} %get-tuple-element.5.gram_ref), custom_call_target="tpu_custom_call" | custom-call | tf_op jit(solution)/shard_map/pallas_call | solution.py:123
  127.7 36.1 %shard_map.61 = (f32[8,256]{1,0:T(8,128)S(1)}, f32[8,2048]{1,0:T(8,128)S(1)}) custom-call(bf16[2048,256]{1,0:T(8,128)(2,1)S(1)} %copy-done, f32[1152,1024]{1,0:T(8,128)S(1)} %shard_map.60.inverse_ref, f32[8,2048]{1,0:T(8,128)S(1)} %copy-done.1, f32[4,8,256]{2,1,0:T(8,128)S(1)} %get-tuple-element.6.first_ref, f32[8,128]{1,0:T(8,128)S(1)} %get-tuple-element.7.norm_ref), custom_call_target="tpu_custom_call" | custom-call | tf_op jit(solution)/shard_map/pallas_call | solution.py:303
  163.8 0.6 copy.8
  164.4 0.6 copy.9
  (1 shorter events, 0.0 us)
Async XLA Ops:
  2.5 1.2 copy-start
  3.7 0.8 copy-start.1
  4.6 0.7 copy-start.2

commit v7 on v6

--- a/solution.py
+++ b/solution.py
@@ -408,8 +408,6 @@
 
     greet(("rows", "cols"))
 
-    share_start("rows", backward_part(right_ref[...], matrix_ref), row_slots, row_send, row_recv)
-
     signs = (1 - 2 * signs_ref[...]).astype(jnp.float32)
 
     def sketch_chunk(target):
@@ -423,11 +421,7 @@
     for place, bit in enumerate(bits):
         start(pieces.at[col], pieces.at[col], piece_send.at[place, col], piece_recv.at[col], {"cols": flip(col, bit)})
 
-    share_finish("rows", row_slots, row_send, row_recv)
-    first_total = added(row_slots)
-    first_norm = jnp.sqrt(first_total[systems:])
-    norm_ref[...] = first_norm[:, :norm_ref.shape[1]]
-    share_start("cols", first_total[:systems] / first_norm, first_ref, col_send, col_recv)
+    share_start("rows", backward_part(right_ref[...], matrix_ref), row_slots, row_send, row_recv)
 
     masks = sorted(range(1, col_size), key=lambda mask: (-(mask & -mask), mask))
 
@@ -469,6 +463,12 @@
                     {"cols": flip(col, bit)},
                 )
         multiply(mask, block)
+
+    share_finish("rows", row_slots, row_send, row_recv)
+    first_total = added(row_slots)
+    first_norm = jnp.sqrt(first_total[systems:])
+    norm_ref[...] = first_norm[:, :norm_ref.shape[1]]
+    share_start("cols", first_total[:systems] / first_norm, first_ref, col_send, col_recv)
 
     block_rows = gram_ref.shape[1] // row_size
 

time: 165 us -> 164 us (level)
  Pallas kernels: 159 us -> 157 us
where the time goes in v7:
time: 164 us
  Pallas kernels  157 us (96%)
  local copies, waits for them, and re-layouts  4.5 us (3%)
    pallas_call x1, Pallas kernels, sketched_gram(): pl.pallas_call(gram_kernel, out_shape=(jax.ShapeDtypeStruct((col_size, st...  80.8 us
    pallas_call x1, Pallas kernels, inverse_factor(): pl.pallas_call(inverse_factor_kernel, out_shape=jax.ShapeDtypeStruct((ord...  40.7 us
    pallas_call x1, Pallas kernels, lsqr(): pl.pallas_call(lsqr_kernel, out_shape=(jax.ShapeDtypeStruct((systems, col...  35.5 us
    unnamed x9, local copies, waits for them, and re-layouts  4.5 us

profile of v7, /device:TPU:0, one launch (start us, length us, event | category | flops | bytes accessed | tf_op | source)
XLA Modules:
  0.0 163.6 jit_solution(12737958971569774178)
XLA Ops:
  0.6 0.5 broadcast.3
  1.1 1.4 reduce.3
  2.5 0.0 copy-start
  2.5 1.2 copy-done
  3.7 0.0 copy-start.1
  3.8 0.8 copy-done.1
  4.6 0.0 copy-start.2
  4.6 0.7 copy-done.2
  5.3 80.8 %shard_map.59 = (f32[4,640,256]{2,1,0:T(8,128)S(1)}, f32[4,8,256]{2,1,0:T(8,128)S(1)}, f32[8,128]{1,0:T(8,128)S(1)}) custom-call(s32[1,2048]{1,0:T(1,128)S(1)} %bitcast.1, s32[8,256]{1,0:T(8,128)S(1)} %reshape.11.sampled_ref, bf16[2048,256]{1,0:T(8,128)(2,1)S(1)} %copy-done, f32[8,2048]{1,0:T(8,128)S(1)} %copy-done.1), custom_call_target="tpu_custom_call" | custom-call | tf_op jit(solution)/shard_map/pallas_call | solution.py:546
  86.1 40.7 %shard_map.60.inverse_ref = f32[1152,1024]{1,0:T(8,128)S(1)} custom-call(f32[4,640,256]{2,1,0:T(8,128)S(1)} %get-tuple-element.5.gram_ref), custom_call_target="tpu_custom_call" | custom-call | tf_op jit(solution)/shard_map/pallas_call | solution.py:123
  126.8 35.5 %shard_map.61 = (f32[8,256]{1,0:T(8,128)S(1)}, f32[8,2048]{1,0:T(8,128)S(1)}) custom-call(bf16[2048,256]{1,0:T(8,128)(2,1)S(1)} %copy-done, f32[1152,1024]{1,0:T(8,128)S(1)} %shard_map.60.inverse_ref, f32[8,2048]{1,0:T(8,128)S(1)} %copy-done.1, f32[4,8,256]{2,1,0:T(8,128)S(1)} %get-tuple-element.6.first_ref, f32[8,128]{1,0:T(8,128)S(1)} %get-tuple-element.7.norm_ref), custom_call_target="tpu_custom_call" | custom-call | tf_op jit(solution)/shard_map/pallas_call | solution.py:303
  162.4 0.6 copy.8
  163.0 0.6 copy.9
  (1 shorter events, 0.0 us)
Async XLA Ops:
  2.5 1.2 copy-start
  3.7 0.8 copy-start.1
  4.6 0.7 copy-start.2
